TPU v7x, 32 devices: a whole 2x2x4 slice. The times are simulated.
32 devices in a mesh: dom: 8 (over z, y), sub: 4 (over x, core).
Axes of the slice: x: 2, y: 2, z: 4, core: 2. Of those that a mesh axis runs over, the one named last changes fastest.
Arguments:
- fields: float32 [6, 20, 32768], P(None, None, ('dom', 'sub')), may hold values from -6 to 6
- geometry: float32 [9, 32768], P(None, ('dom', 'sub')), may hold values from -4 to 4
- normals: float32 [3, 4, 32768], P(None, None, ('dom', 'sub')), may hold values from -3 to 3
- face_scale: float32 [4, 32768], P(None, ('dom', 'sub')), may hold values from 0.5 to 3
- derivatives: float32 [3, 20, 20], replicated, may hold values from -1.25 to 1.25
- lift_matrix: float32 [20, 40], replicated, may hold values from -1 to 1
- face_nbr: int32 [4, 32768], P(None, ('dom', 'sub')), may hold values from 0 to 4607, as said below
- send_rows: int32 [16384], P(('dom', 'sub')), may hold values from 64 to 1024, as said below
- fine_slots: int32 [4096], P(('dom', 'sub')), may hold values from 0 to 511, as said below
- export_rows: int32 [2, 512], P(None, ('dom', 'sub')), may hold values from 0 to 127, as said below
- fine_nbr: int32 [4, 4096], P(None, ('dom', 'sub')), may hold values from 0 to 640
Outputs:
- fields_out: float32 [6, 20, 32768], P(None, None, ('dom', 'sub'))
Inputs may be any that keep to these rules, and one draw needn't show every extreme that they name: `face_nbr`: A wall face holds its own number 4 (e - p * 1024) + f. Codes from 4096 up occur only on the first 64 and the last 64 elements of a device: the first 64 use 4 * 1024 to 4351, the last 64 use 4 * 1024 + 4 * 64 and above. `send_rows`: entry p * 512 + j * 64 + c is the row within device p of the c-th element that p hands to the device of dom index j and p's sub index; 1024 marks an empty slot, and filled slots come first in each group of 64. Each group holds 0, 32 or 64 elements; in each sub index half of the dom indices hand 2 * 128 elements each, each of them 64 to some device, the others hand none. Handed rows are distinct and lie in 64 to 959. `fine_slots`: the 128 entries of a device are the filled slots j * 64 + c addressed to it (j the sender's dom index), each exactly once, in some order. `export_rows`: each row of a device holds 16 distinct positions among its 128 fine elements.
All inputs are finite; a program needn't handle non-finite values.
Results may differ from a plain program's by a relative error of at most 0.0001.
Values sent between devices are 32-bit elements; how exact they have to be, the bound alone decides.
A program may use at most 128 MiB of HBM per device.

v0:
```python
import functools

import jax
import jax.numpy as jnp
import numpy as np
from jax import lax
from jax.experimental import pallas as pl
from jax.experimental.pallas import tpu as pltpu
from jax.sharding import PartitionSpec as P

SUBSTEPS = 4
coarse_step = 0.2

PADC = 24
FR = 80
FN = 16
TR = 192
PK = 384
RK = 128
GEO, NS, CODE = 0, 9, 24
CHUNK = 256

bf16 = jnp.bfloat16
f32 = jnp.float32
MESH = pl.DeviceIdType.MESH


def face_table():
    places = [
        (along_r, along_s, along_t)
        for along_t in range(4)
        for along_s in range(4 - along_t)
        for along_r in range(4 - along_t - along_s)
    ]
    bottom_face = [number for number, location in enumerate(places) if location[2] == 0]
    front_face = [number for number, location in enumerate(places) if location[1] == 0]
    slanted = [number for number, location in enumerate(places) if sum(location) == 3]
    beside = [number for number, location in enumerate(places) if location[0] == 0]
    return np.array([bottom_face, front_face, slanted, beside], dtype=np.int32).T


def tables():
    nodes = face_table()
    sel = np.zeros((TR, 2 * FR), np.float32)
    pack = np.zeros((368, 4 * FR + 4 * TR), np.float32)
    unpack = np.zeros((2 * FR + 2 * TR, 2 * PK), np.float32)
    ret = np.zeros((RK, 4 * FR), np.float32)
    back = np.zeros((2 * FR, 2 * RK), np.float32)
    for c in range(3):
        for p in range(20):
            for field in range(2):
                packed = (field * 3 + c) * 20 + p
                for s in range(2):
                    at = field * 2 * FR + s * FR + c * PADC + p
                    pack[packed, at] = 1
                    ret[packed, at] = 1
                    unpack[field * FR + c * PADC + p, s * PK + packed] = 1
                    back[field * FR + c * PADC + p, s * RK + packed] = 1
        for f in range(4):
            for n in range(10):
                row = f * 3 * FN + c * FN + n
                for s in range(2):
                    sel[row, s * FR + c * PADC + nodes[n, f]] = 1
                for field in range(2):
                    packed = 120 + field * 120 + (f * 3 + c) * 10 + n
                    for s in range(2):
                        pack[packed, 4 * FR + field * 2 * TR + s * TR + row] = 1
                        unpack[2 * FR + field * TR + row, s * PK + packed] = 1
    d_rows = np.zeros((3, 224, 20), np.float32)
    d_hi = np.zeros((20, 3 * FR), np.float32)
    d_lo = np.zeros((20, 3 * FR), np.float32)
    d_mask = np.zeros((224, 3 * FR), np.float32)
    l_rows = np.zeros((FR, 20), np.float32)
    l_hi = np.zeros((40, 3 * TR), np.float32)
    l_lo = np.zeros((40, 3 * TR), np.float32)
    l_mask = np.zeros((FR, 3 * TR), np.float32)
    for c in range(3):
        for p in range(20):
            l_rows[c * PADC + p, p] = 1
            for a in range(3):
                d_rows[a, (a * 3 + c) * PADC + p, p] = 1
            d_hi[p, c * PADC + p] = 1
            d_hi[p, FR + c * PADC + p] = 1
            d_lo[p, 2 * FR + c * PADC + p] = 1
        for s in range(3):
            for a in range(3):
                at = (a * 3 + c) * PADC
                d_mask[at : at + 20, s * FR + c * PADC : s * FR + c * PADC + 20] = 1
            for f in range(4):
                col = s * TR + f * 3 * FN + c * FN
                l_mask[c * PADC : c * PADC + 20, col : col + 10] = 0.5
                for n in range(10):
                    (l_lo if s == 2 else l_hi)[f * 10 + n, col + n] = 1
    out = [sel, pack, unpack, ret, back, d_rows, d_hi, d_lo, l_rows, l_hi, l_lo]
    return [x.astype(jnp.bfloat16) for x in out] + [d_mask, l_mask]


def split(x):
    hi = x.astype(bf16).astype(f32)
    return hi, x - hi


def split2(x):
    hi, lo = split(x)
    return jnp.concatenate([hi, lo], axis=0).astype(bf16)


def split3(x):
    hi, lo = split(x)
    return jnp.concatenate([hi, lo, hi], axis=0).astype(bf16)


def dot(a, b):
    return jnp.dot(a, b, preferred_element_type=f32)


def dot_t(a, b):
    return lax.dot_general(a, b, (((1,), (1,)), ((), ())), preferred_element_type=f32)


def one_hot(count, row):
    at = lax.broadcasted_iota(jnp.int32, (count, row.shape[1]), 0)
    return jnp.where(at == row, 1.0, 0.0).astype(bf16)


def curl(grad, geo):
    def partial(m, c):
        total = None
        for a in range(3):
            at = (a * 3 + c) * PADC
            term = geo[3 * m + a : 3 * m + a + 1] * grad[at : at + PADC]
            total = term if total is None else total + term
        return total

    parts = [
        partial(1, 2) - partial(2, 1),
        partial(2, 0) - partial(0, 2),
        partial(0, 1) - partial(1, 0),
    ]
    pad = jnp.zeros((FR - 3 * PADC, grad.shape[1]), f32)
    return jnp.concatenate([*parts, pad], axis=0)


def pick_face(traces, face):
    total = traces[: 3 * FN]
    for g in range(1, 4):
        total = jnp.where(face == g, traces[g * 3 * FN : (g + 1) * 3 * FN], total)
    return total


def flux(jump, ns, f):
    n = [ns[c * 4 + f : c * 4 + f + 1] for c in range(3)]
    j = [jump[c * FN : (c + 1) * FN] for c in range(3)]
    return [
        n[1] * j[2] - n[2] * j[1],
        n[2] * j[0] - n[0] * j[2],
        n[0] * j[1] - n[1] * j[0],
    ]


def kernel(
    n_dom,
    n_sub,
    width,
    fields,
    geometry,
    normals,
    face_scale,
    derivatives,
    lift_matrix,
    face_nbr,
    send_rows,
    fine_slots,
    export_row,
    fine_nbr,
    sel,
    pack,
    unpack,
    ret,
    back,
    d_rows,
    d_hi,
    d_lo,
    l_rows,
    l_hi,
    l_lo,
    d_mask,
    l_mask,
    out,
    own_e,
    own_h,
    pool_e,
    pool_h,
    stat,
    send_hot,
    fine_own,
    fine_halo,
    dmat,
    lmat,
    hand_out,
    hand_in,
    back_out,
    back_in,
    fine_out,
    fine_in,
    halo_out,
    halo_in,
    hand_send,
    hand_recv,
    back_send,
    back_recv,
    fine_send,
    fine_recv,
    halo_send,
    halo_recv,
):
    count = fields.shape[2]
    fine = fine_slots.shape[1]
    cap = hand_out.shape[1]
    slots = n_dom * cap
    dom, sub = lax.axis_index("dom"), lax.axis_index("sub")
    me = dom * n_sub + sub
    total = n_dom * n_sub
    after, before = lax.rem(me + 1, total), lax.rem(me + total - 1, total)
    after_id = (after // n_sub, lax.rem(after, n_sub))
    before_id = (before // n_sub, lax.rem(before, n_sub))

    barrier = pltpu.get_barrier_semaphore()
    for target in (after_id, before_id):
        pl.semaphore_signal(barrier, inc=1, device_id=target, device_id_type=MESH)

    @pl.loop(1, n_dom)
    def _(i):
        pl.semaphore_signal(
            barrier, inc=1, device_id=(lax.rem(dom + i, n_dom), sub), device_id_type=MESH
        )

    for ref, first in ((own_e, 0), (own_h, 3)):
        ref[...] = jnp.zeros(ref.shape, f32)
        for c in range(3):
            ref[c * PADC : c * PADC + 20, :] = fields[first + c]
    pool_e[:, :count] = split2(own_e[...])
    pool_h[:, :count] = split2(own_h[...])
    stat[...] = jnp.zeros(stat.shape, f32)
    stat[GEO : GEO + 9, :] = geometry[...]
    for c in range(3):
        stat[NS + 4 * c : NS + 4 * c + 4, :] = normals[c] * face_scale[...]
    stat[CODE : CODE + 4, :] = face_nbr[...].astype(f32)

    halo_out[0, 0] = own_e[:, count - 128 :]
    halo_out[0, 1] = own_e[:, :128]

    rows = send_rows[...]
    hot = one_hot(count, rows)
    send_hot[...] = hot
    picked_e = dot(pool_e[:, :count], hot).astype(bf16)
    picked_h = dot(pool_h[:, :count], hot).astype(bf16)
    picked_stat = dot(split2(stat[...]), hot)
    picked_stat = picked_stat[:32] + picked_stat[32:]
    traces_e = dot(sel[...], picked_e)
    traces_h = dot(sel[...], picked_h)
    held_e, held_h = [], []
    for f in range(4):
        code = picked_stat[CODE + f : CODE + f + 1].astype(jnp.int32)
        near = one_hot(count, code >> 2)
        face = code & 3
        wall = code == 4 * rows + f
        e = pick_face(dot(sel[...], dot(pool_e[:, :count], near).astype(bf16)), face)
        h = pick_face(dot(sel[...], dot(pool_h[:, :count], near).astype(bf16)), face)
        at = f * 3 * FN
        held_e.append(jnp.where(wall, -traces_e[at : at + 3 * FN], e))
        held_h.append(jnp.where(wall, traces_h[at : at + 3 * FN], h))
    everything = jnp.concatenate(
        [
            picked_e,
            picked_h,
            split2(jnp.concatenate(held_e, axis=0)),
            split2(jnp.concatenate(held_h, axis=0)),
        ],
        axis=0,
    )
    packed = jnp.concatenate([dot(pack[...], everything)[:360], picked_stat[:24]], axis=0)
    hand_out[...] = packed.T.reshape(n_dom, cap, PK)

    pl.semaphore_wait(barrier, n_dom + 1)

    def exchange(src, dst, send, recv):
        def copy(i):
            target = lax.rem(dom + i, n_dom)
            return pltpu.make_async_remote_copy(
                src_ref=src.at[target],
                dst_ref=dst.at[dom],
                send_sem=send.at[i],
                recv_sem=recv.at[i],
                device_id=(target, sub),
                device_id_type=MESH,
            )

        @pl.loop(1, n_dom)
        def _(i):
            copy(i).start()

        dst[pl.ds(dom, 1)] = src[pl.ds(dom, 1)]
        return copy

    def finish(copy):
        @pl.loop(1, n_dom)
        def _(i):
            copy(i).wait()

    def to_neighbours(src_up, src_down, dst, send, recv):
        copies = []
        for side, (src, target) in enumerate(((src_up, after_id), (src_down, before_id))):
            copy = pltpu.make_async_remote_copy(
                src_ref=src,
                dst_ref=dst.at[side],
                send_sem=send.at[side],
                recv_sem=recv.at[side],
                device_id=target,
                device_id_type=MESH,
            )
            copy.start()
            copies.append(copy)
        return copies

    handed = exchange(hand_out, hand_in, hand_send, hand_recv)
    halo_e = to_neighbours(
        halo_out.at[0, 0], halo_out.at[0, 1], halo_in.at[0], halo_send.at[0], halo_recv.at[0]
    )

    rows_hi = rows_lo = None
    for a in range(3):
        hi, lo = split(derivatives[a])
        hi = dot(d_rows[a], hi.astype(bf16))
        lo = dot(d_rows[a], lo.astype(bf16))
        rows_hi = hi if a == 0 else rows_hi + hi
        rows_lo = lo if a == 0 else rows_lo + lo
    wide = dot(rows_hi.astype(bf16), d_hi[...]) + dot(rows_lo.astype(bf16), d_lo[...])
    dmat[...] = (wide * d_mask[...]).astype(bf16)
    hi, lo = split(lift_matrix[...])
    hi = dot(l_rows[...], hi.astype(bf16))
    lo = dot(l_rows[...], lo.astype(bf16))
    wide = dot(hi.astype(bf16), l_hi[...]) + dot(lo.astype(bf16), l_lo[...])
    lmat[...] = (wide * l_mask[...]).astype(bf16)

    codes = [fine_nbr[f : f + 1, :] for f in range(4)]
    code_row = jnp.concatenate(codes, axis=1) >> 2
    fine_own[...] = one_hot(fine, code_row)
    fine_halo[...] = one_hot(128, code_row - fine)
    export_hot = one_hot(fine, export_row[...])
    slot_hot = one_hot(slots, fine_slots[...])

    finish(handed)
    received = hand_in[...].reshape(slots, PK).T
    received = dot(split2(received), slot_hot)
    fine_stat = received[360:384] + received[PK + 360 : PK + 384]
    state = dot(unpack[...], received.astype(bf16))
    efield, hfield = state[:FR], state[FR : 2 * FR]
    fine_held = (state[2 * FR : 2 * FR + TR], state[2 * FR + TR :])
    fine_geo, fine_ns = fine_stat[GEO : GEO + 9], fine_stat[NS : NS + 12]
    lane = lax.broadcasted_iota(jnp.int32, (FR, 128), 1)
    frozen_code = 4 * fine + 8 * width

    def fine_rate(field, held, turn):
        parts = split2(field)
        export = dot(parts, export_hot)
        fine_out[turn] = export[:FR] + export[FR:]
        copies = to_neighbours(
            fine_out.at[turn], fine_out.at[turn], fine_in.at[turn], fine_send.at[turn], fine_recv.at[turn]
        )
        near = dot(parts, fine_own[...])
        own = dot(sel[...], parts)
        spin = curl(dot(dmat[...], split3(field)), fine_geo)
        for copy in copies:
            copy.wait()
        halo = jnp.where(lane < width, fine_in[turn, 0], fine_in[turn, 1])
        near = near + dot(split2(halo), fine_halo[...])
        traces = dot(sel[...], near.astype(bf16))
        fluxes = []
        for f in range(4):
            at = f * 3 * FN
            outside = pick_face(traces[:, f * fine : (f + 1) * fine], codes[f] & 3)
            outside = jnp.where(codes[f] == frozen_code, held[at : at + 3 * FN], outside)
            fluxes += flux(outside - own[at : at + 3 * FN], fine_ns, f)
        return spin + dot(lmat[...], split3(jnp.concatenate(fluxes, axis=0)))

    fine_step = coarse_step / SUBSTEPS
    for substep in range(SUBSTEPS):
        hfield = hfield - fine_step * fine_rate(efield, fine_held[0], 2 * substep)
        efield = efield + fine_step * fine_rate(hfield, fine_held[1], 2 * substep + 1)

    result = jnp.concatenate([split2(efield), split2(hfield)], axis=0)
    result = split2(dot(ret[...], result))
    result = dot_t(slot_hot, result)
    result = result[:, :RK] + result[:, RK:]
    back_out[...] = result.reshape(n_dom, cap, RK)
    returned = exchange(back_out, back_in, back_send, back_recv)
    is_fine = dot_t(jnp.ones((16, slots), bf16), send_hot[...])[:1] > 0.5
    finish(returned)
    came = back_in[...].reshape(slots, RK).T
    came = dot_t(split2(came), send_hot[...]).astype(bf16)
    came = dot(back[...], came)
    merged_e = jnp.where(is_fine, came[:FR], own_e[...])
    merged_h = jnp.where(is_fine, came[FR:], own_h[...])
    own_e[...] = merged_e
    own_h[...] = merged_h
    pool_e[:, :count] = split2(merged_e)

    halo_lane = lax.broadcasted_iota(jnp.int32, (FR, 128), 1)
    place = lax.broadcasted_iota(jnp.int32, (1, CHUNK), 1)

    def coarse_rate(start, source, pool, reach, mirror):
        window = pl.ds(start, CHUNK)
        field = source[:, window]
        table = stat[:, window]
        spin = curl(dot(dmat[...], split3(field)), table[GEO : GEO + 9])
        own = dot(sel[...], split2(field))
        ns = table[NS : NS + 12]
        fluxes = []
        for f in range(4):
            code = face_nbr[f : f + 1, window]
            near = dot(pool[:, :reach], one_hot(reach, code >> 2)).astype(bf16)
            outside = pick_face(dot(sel[...], near), code & 3)
            mine = own[f * 3 * FN : (f + 1) * 3 * FN]
            wall = code == 4 * (start + place) + f
            outside = jnp.where(wall, mirror * mine, outside)
            fluxes += flux(outside - mine, ns, f)
        return spin + dot(lmat[...], split3(jnp.concatenate(fluxes, axis=0)))

    def set_halo(pool, turn, copies):
        for copy in copies:
            copy.wait()
        tile = jnp.where(halo_lane < 64, halo_in[turn, 1], halo_in[turn, 0])
        pool[:, count:] = split2(pltpu.roll(tile, 64, 1))

    def update(start, source, pool, target, first, scale, reach, mirror):
        start = pl.multiple_of(start, CHUNK)
        window = pl.ds(start, CHUNK)
        new = target[:, window] + scale * coarse_rate(start, source, pool, reach, mirror)
        target[:, window] = new
        for c in range(3):
            out[first + c, :, window] = new[c * PADC : c * PADC + 20]
        if first == 3:
            pool_h[:, window] = split2(new)

    last = count - CHUNK
    full = count + 128
    set_halo(pool_e, 0, halo_e)

    @pl.loop(0, 2)
    def _(i):
        update(i * last, own_e, pool_e, own_h, 3, -coarse_step, full, -1.0)

    halo_out[1, 0] = own_h[:, count - 128 :]
    halo_out[1, 1] = own_h[:, :128]
    halo_h = to_neighbours(
        halo_out.at[1, 0], halo_out.at[1, 1], halo_in.at[1], halo_send.at[1], halo_recv.at[1]
    )

    @pl.loop(1, count // CHUNK - 1)
    def _(i):
        update(i * CHUNK, own_e, pool_e, own_h, 3, -coarse_step, count, -1.0)

    @pl.loop(1, count // CHUNK - 1)
    def _(i):
        update(i * CHUNK, own_h, pool_h, own_e, 0, coarse_step, count, 1.0)

    set_halo(pool_h, 1, halo_h)

    @pl.loop(0, 2)
    def _(i):
        update(i * last, own_h, pool_h, own_e, 0, coarse_step, full, 1.0)


def per_device(
    n_dom,
    n_sub,
    fields,
    geometry,
    normals,
    face_scale,
    derivatives,
    lift_matrix,
    face_nbr,
    send_rows,
    fine_slots,
    export_rows,
    fine_nbr,
):
    count = fields.shape[2]
    fine = fine_slots.shape[0]
    width = export_rows.shape[1]
    group = send_rows.shape[0] // n_dom
    cap = -(-group // 8) * 8
    slots = n_dom * cap
    turns = 2 * SUBSTEPS
    if cap != group:
        send_rows = jnp.pad(
            send_rows.reshape(n_dom, group),
            ((0, 0), (0, cap - group)),
            constant_values=count,
        ).reshape(-1)
        fine_slots = fine_slots // group * cap + fine_slots % group
    export_row = jnp.concatenate(
        [export_rows[1], export_rows[0], jnp.full((128 - 2 * width,), -1, jnp.int32)]
    )
    operands = [
        fields,
        geometry,
        normals,
        face_scale,
        derivatives,
        lift_matrix,
        face_nbr,
        send_rows[None],
        fine_slots[None],
        export_row[None],
        fine_nbr,
        *[jnp.asarray(x) for x in tables()],
    ]
    vmem = pl.BlockSpec(memory_space=pltpu.VMEM)
    dma = pltpu.SemaphoreType.DMA
    return pl.pallas_call(
        functools.partial(kernel, n_dom, n_sub, width),
        out_shape=jax.ShapeDtypeStruct(fields.shape, f32),
        in_specs=[vmem] * len(operands),
        out_specs=vmem,
        scratch_shapes=[
            pltpu.VMEM((FR, count), f32),
            pltpu.VMEM((FR, count), f32),
            pltpu.VMEM((2 * FR, count + 128), bf16),
            pltpu.VMEM((2 * FR, count + 128), bf16),
            pltpu.VMEM((32, count), f32),
            pltpu.VMEM((count, slots), bf16),
            pltpu.VMEM((fine, 4 * fine), bf16),
            pltpu.VMEM((128, 4 * fine), bf16),
            pltpu.VMEM((224, 3 * FR), bf16),
            pltpu.VMEM((FR, 3 * TR), bf16),
            pltpu.VMEM((n_dom, cap, PK), f32),
            pltpu.VMEM((n_dom, cap, PK), f32),
            pltpu.VMEM((n_dom, cap, RK), f32),
            pltpu.VMEM((n_dom, cap, RK), f32),
            pltpu.VMEM((turns, FR, 128), f32),
            pltpu.VMEM((turns, 2, FR, 128), f32),
            pltpu.VMEM((2, 2, FR, 128), f32),
            pltpu.VMEM((2, 2, FR, 128), f32),
            dma((n_dom,)),
            dma((n_dom,)),
            dma((n_dom,)),
            dma((n_dom,)),
            dma((turns, 2)),
            dma((turns, 2)),
            dma((2, 2)),
            dma((2, 2)),
        ],
        compiler_params=pltpu.CompilerParams(
            collective_id=0, has_side_effects=True, vmem_limit_bytes=56 * 1024 * 1024
        ),
    )(*operands)


def solution(mesh):
    return jax.shard_map(
        functools.partial(per_device, mesh.shape["dom"], mesh.shape["sub"]),
        mesh=mesh,
        in_specs=(
            P(None, None, ("dom", "sub")),
            P(None, ("dom", "sub")),
            P(None, None, ("dom", "sub")),
            P(None, ("dom", "sub")),
            P(),
            P(),
            P(None, ("dom", "sub")),
            P(("dom", "sub")),
            P(("dom", "sub")),
            P(None, ("dom", "sub")),
            P(None, ("dom", "sub")),
        ),
        out_specs=P(None, None, ("dom", "sub")),
        check_vma=False,
    )
```

profile of v0, /device:TPU:0, one launch (start us, length us, event | category | flops | bytes accessed | tf_op | source)
XLA Modules:
  0.0 92.4 jit_solution(8272724222360032249)
XLA Ops:
  0.0 0.0 copy-start
  0.0 0.7 copy-done
  0.7 0.6 add_bitcast_fusion.export_row
  1.3 89.1 %shard_map.226 = f32[6,20,1024]{2,1,0:T(8,128)} custom-call(f32[6,20,1024]{2,1,0:T(8,128)} %fields.1, f32[9,1024]{1,0:T(8,128)} %geometry.1, f32[3,4,1024]{2,1,0:T(4,128)} %normals.1, f32[4,1024]{1,0:T(4,128)} %face_scale.1, f32[3,20,20]{2,1,0:T(8,128)} %derivatives.1, f32[20,40]{1,0:T(8,128)} %lift_matrix.1, s32[4,1024]{1,0:T(4,128)} %face_nbr.1, ...), custom_call_target="tpu_custom_call" | custom-call | tf_op jit(solution)/shard_map/pallas_call | solution.py:523
  90.4 1.9 %copy.26 = f32[6,20,1024]{2,1,0:T(8,128)} copy(f32[6,20,1024]{2,1,0:T(8,128)} %shard_map.226) | data formatting | bytes 983040
  (2 shorter events, 0.0 us)
Async XLA Ops:
  0.0 0.7 copy-start
where the time goes:
time: 92.9 us; the launch traced here: 92.4 us
  Pallas kernels  89.1 us (96%)
  local copies, waits for them, and re-layouts  2.61 us (3%)
    pallas_call x1, Pallas kernels, per_device(): pl.pallas_call(functools.partial(kernel, n_dom, n_sub, width), out_shape=...  89.1 us
    unnamed x3, local copies, waits for them, and re-layouts  2.61 us

commit v1 on v0

--- a/solution.py
+++ b/solution.py
@@ -15,7 +15,6 @@
 FR = 80
 FN = 16
 TR = 192
-PK = 384
 RK = 128
 GEO, NS, CODE = 0, 9, 24
 CHUNK = 256
@@ -42,30 +41,19 @@
 def tables():
     nodes = face_table()
     sel = np.zeros((TR, 2 * FR), np.float32)
-    pack = np.zeros((368, 4 * FR + 4 * TR), np.float32)
-    unpack = np.zeros((2 * FR + 2 * TR, 2 * PK), np.float32)
-    ret = np.zeros((RK, 4 * FR), np.float32)
-    back = np.zeros((2 * FR, 2 * RK), np.float32)
+    pack = np.zeros((RK, 4 * FR), np.float32)
+    unpack = np.zeros((2 * FR, 2 * RK), np.float32)
     for c in range(3):
         for p in range(20):
             for field in range(2):
                 packed = (field * 3 + c) * 20 + p
                 for s in range(2):
-                    at = field * 2 * FR + s * FR + c * PADC + p
-                    pack[packed, at] = 1
-                    ret[packed, at] = 1
-                    unpack[field * FR + c * PADC + p, s * PK + packed] = 1
-                    back[field * FR + c * PADC + p, s * RK + packed] = 1
+                    pack[packed, field * 2 * FR + s * FR + c * PADC + p] = 1
+                    unpack[field * FR + c * PADC + p, s * RK + packed] = 1
         for f in range(4):
             for n in range(10):
-                row = f * 3 * FN + c * FN + n
                 for s in range(2):
-                    sel[row, s * FR + c * PADC + nodes[n, f]] = 1
-                for field in range(2):
-                    packed = 120 + field * 120 + (f * 3 + c) * 10 + n
-                    for s in range(2):
-                        pack[packed, 4 * FR + field * 2 * TR + s * TR + row] = 1
-                        unpack[2 * FR + field * TR + row, s * PK + packed] = 1
+                    sel[f * 3 * FN + c * FN + n, s * FR + c * PADC + nodes[n, f]] = 1
     d_rows = np.zeros((3, 224, 20), np.float32)
     d_hi = np.zeros((20, 3 * FR), np.float32)
     d_lo = np.zeros((20, 3 * FR), np.float32)
@@ -91,7 +79,7 @@
                 l_mask[c * PADC : c * PADC + 20, col : col + 10] = 0.5
                 for n in range(10):
                     (l_lo if s == 2 else l_hi)[f * 10 + n, col + n] = 1
-    out = [sel, pack, unpack, ret, back, d_rows, d_hi, d_lo, l_rows, l_hi, l_lo]
+    out = [sel, pack, unpack, d_rows, d_hi, d_lo, l_rows, l_hi, l_lo]
     return [x.astype(jnp.bfloat16) for x in out] + [d_mask, l_mask]
 
 
@@ -171,13 +159,11 @@
     face_nbr,
     send_rows,
     fine_slots,
-    export_row,
+    export_rows,
     fine_nbr,
     sel,
     pack,
     unpack,
-    ret,
-    back,
     d_rows,
     d_hi,
     d_lo,
@@ -189,14 +175,19 @@
     out,
     own_e,
     own_h,
-    pool_e,
-    pool_h,
+    pool,
     stat,
+    frozen,
     send_hot,
+    coarse_hot,
     fine_own,
     fine_halo,
     dmat,
     lmat,
+    mask_out,
+    mask_in,
+    extra_out,
+    extra_in,
     hand_out,
     hand_in,
     back_out,
@@ -205,6 +196,10 @@
     fine_in,
     halo_out,
     halo_in,
+    mask_send,
+    mask_recv,
+    extra_send,
+    extra_recv,
     hand_send,
     hand_recv,
     back_send,
@@ -216,8 +211,9 @@
 ):
     count = fields.shape[2]
     fine = fine_slots.shape[1]
-    cap = hand_out.shape[1]
+    cap = hand_out.shape[2]
     slots = n_dom * cap
+    full = count + 128
     dom, sub = lax.axis_index("dom"), lax.axis_index("sub")
     me = dom * n_sub + sub
     total = n_dom * n_sub
@@ -234,55 +230,6 @@
         pl.semaphore_signal(
             barrier, inc=1, device_id=(lax.rem(dom + i, n_dom), sub), device_id_type=MESH
         )
-
-    for ref, first in ((own_e, 0), (own_h, 3)):
-        ref[...] = jnp.zeros(ref.shape, f32)
-        for c in range(3):
-            ref[c * PADC : c * PADC + 20, :] = fields[first + c]
-    pool_e[:, :count] = split2(own_e[...])
-    pool_h[:, :count] = split2(own_h[...])
-    stat[...] = jnp.zeros(stat.shape, f32)
-    stat[GEO : GEO + 9, :] = geometry[...]
-    for c in range(3):
-        stat[NS + 4 * c : NS + 4 * c + 4, :] = normals[c] * face_scale[...]
-    stat[CODE : CODE + 4, :] = face_nbr[...].astype(f32)
-
-    halo_out[0, 0] = own_e[:, count - 128 :]
-    halo_out[0, 1] = own_e[:, :128]
-
-    rows = send_rows[...]
-    hot = one_hot(count, rows)
-    send_hot[...] = hot
-    picked_e = dot(pool_e[:, :count], hot).astype(bf16)
-    picked_h = dot(pool_h[:, :count], hot).astype(bf16)
-    picked_stat = dot(split2(stat[...]), hot)
-    picked_stat = picked_stat[:32] + picked_stat[32:]
-    traces_e = dot(sel[...], picked_e)
-    traces_h = dot(sel[...], picked_h)
-    held_e, held_h = [], []
-    for f in range(4):
-        code = picked_stat[CODE + f : CODE + f + 1].astype(jnp.int32)
-        near = one_hot(count, code >> 2)
-        face = code & 3
-        wall = code == 4 * rows + f
-        e = pick_face(dot(sel[...], dot(pool_e[:, :count], near).astype(bf16)), face)
-        h = pick_face(dot(sel[...], dot(pool_h[:, :count], near).astype(bf16)), face)
-        at = f * 3 * FN
-        held_e.append(jnp.where(wall, -traces_e[at : at + 3 * FN], e))
-        held_h.append(jnp.where(wall, traces_h[at : at + 3 * FN], h))
-    everything = jnp.concatenate(
-        [
-            picked_e,
-            picked_h,
-            split2(jnp.concatenate(held_e, axis=0)),
-            split2(jnp.concatenate(held_h, axis=0)),
-        ],
-        axis=0,
-    )
-    packed = jnp.concatenate([dot(pack[...], everything)[:360], picked_stat[:24]], axis=0)
-    hand_out[...] = packed.T.reshape(n_dom, cap, PK)
-
-    pl.semaphore_wait(barrier, n_dom + 1)
 
     def exchange(src, dst, send, recv):
         def copy(i):
@@ -308,11 +255,11 @@
         def _(i):
             copy(i).wait()
 
-    def to_neighbours(src_up, src_down, dst, send, recv):
+    def to_neighbours(src, dst, send, recv):
         copies = []
-        for side, (src, target) in enumerate(((src_up, after_id), (src_down, before_id))):
+        for side, target in enumerate((after_id, before_id)):
             copy = pltpu.make_async_remote_copy(
-                src_ref=src,
+                src_ref=src.at[side],
                 dst_ref=dst.at[side],
                 send_sem=send.at[side],
                 recv_sem=recv.at[side],
@@ -323,10 +270,57 @@
             copies.append(copy)
         return copies
 
-    handed = exchange(hand_out, hand_in, hand_send, hand_recv)
-    halo_e = to_neighbours(
-        halo_out.at[0, 0], halo_out.at[0, 1], halo_in.at[0], halo_send.at[0], halo_recv.at[0]
-    )
+    def slots_of(d, row):
+        at = lax.broadcasted_iota(jnp.int32, (128, row.shape[1]), 0)
+        return jnp.where((row - d * cap == at) & (at < cap), 1.0, 0.0).astype(bf16)
+
+    codes = [fine_nbr[f : f + 1, :] for f in range(4)]
+    frozen_code = 4 * fine + 8 * width
+    frozen[...] = jnp.zeros(frozen.shape, f32)
+    frozen[0:4, :] = jnp.where(fine_nbr[...] == frozen_code, 1.0, 0.0)
+    my_slots = fine_slots[...]
+
+    @pl.loop(0, n_dom)
+    def _(d):
+        mask_out[d] = dot_t(frozen[...].astype(bf16), slots_of(d, my_slots))[:8]
+
+    for ref, first in ((own_e, 0), (own_h, 3)):
+        ref[...] = jnp.zeros(ref.shape, f32)
+        for c in range(3):
+            ref[c * PADC : c * PADC + 20, :] = fields[first + c]
+    halo_out[0, 0] = own_e[:, count - 128 :]
+    halo_out[0, 1] = own_e[:, :128]
+
+    pl.semaphore_wait(barrier, n_dom + 1)
+    masks = exchange(mask_out, mask_in, mask_send, mask_recv)
+    halo_e = to_neighbours(halo_out.at[0], halo_in.at[0], halo_send.at[0], halo_recv.at[0])
+
+    stat[...] = jnp.zeros(stat.shape, f32)
+    stat[GEO : GEO + 9, :] = geometry[...]
+    for c in range(3):
+        stat[NS + 4 * c : NS + 4 * c + 4, :] = normals[c] * face_scale[...]
+    stat[CODE : CODE + 4, :] = face_nbr[...].astype(f32)
+    pool[: 2 * FR, :count] = split2(own_e[...])
+    pool[2 * FR : 4 * FR, :count] = split2(own_h[...])
+    pool[4 * FR :, :count] = split2(stat[...])
+
+    rows = send_rows[...]
+    send_hot[...] = one_hot(count, rows)
+    picked = dot(pool[:, :count], send_hot[...])
+    slot_stat = picked[4 * FR : 4 * FR + 32] + picked[4 * FR + 32 :]
+    picked = picked[: 4 * FR].astype(bf16)
+    message = jnp.concatenate([dot(pack[...], picked)[:120], slot_stat[:8]], axis=0)
+    hand_out[0] = message.T.reshape(n_dom, cap, RK)
+    handed_fields = exchange(hand_out.at[0], hand_in.at[0], hand_send.at[0], hand_recv.at[0])
+    slot_row = lax.broadcasted_iota(jnp.int32, (1, slots), 1)
+    extra = split2(slot_stat[16:24])
+
+    @pl.loop(0, n_dom)
+    def _(d):
+        part = dot_t(extra, slots_of(d, slot_row))
+        extra_out[d] = part[:8] + part[8:]
+
+    extras = exchange(extra_out, extra_in, extra_send, extra_recv)
 
     rows_hi = rows_lo = None
     for a in range(3):
@@ -343,54 +337,103 @@
     wide = dot(hi.astype(bf16), l_hi[...]) + dot(lo.astype(bf16), l_lo[...])
     lmat[...] = (wide * l_mask[...]).astype(bf16)
 
-    codes = [fine_nbr[f : f + 1, :] for f in range(4)]
+    traces_e = dot(sel[...], picked[: 2 * FR])
+    traces_h = dot(sel[...], picked[2 * FR :])
+    held_e, held_h = [], []
+    for f in range(4):
+        code = slot_stat[CODE + f : CODE + f + 1].astype(jnp.int32)
+        face = code & 3
+        wall = code == 4 * rows + f
+        near = dot(pool[: 4 * FR, :count], one_hot(count, code >> 2)).astype(bf16)
+        e = pick_face(dot(sel[...], near[: 2 * FR]), face)
+        h = pick_face(dot(sel[...], near[2 * FR :]), face)
+        at = f * 3 * FN
+        held_e.append(jnp.where(wall, -traces_e[at : at + 3 * FN], e))
+        held_h.append(jnp.where(wall, traces_h[at : at + 3 * FN], h))
+    finish(masks)
+
+    def add_mask(d, mask):
+        part = jnp.concatenate([mask_in[d], jnp.zeros((8, 128), f32)], axis=0).astype(bf16)
+        return mask + dot(part, slots_of(d, slot_row))
+
+    mask = lax.fori_loop(0, n_dom, add_mask, jnp.zeros((16, slots), f32))
+    kept_e, kept_h = [], []
+    for f in range(4):
+        keep = mask[f : f + 1] > 0.5
+        kept_e += flux(jnp.where(keep, held_e[f], 0.0), slot_stat[NS : NS + 12], f)
+        kept_h += flux(jnp.where(keep, held_h[f], 0.0), slot_stat[NS : NS + 12], f)
+    kept_e = dot(lmat[...], split3(jnp.concatenate(kept_e, axis=0)))
+    kept_h = dot(lmat[...], split3(jnp.concatenate(kept_h, axis=0)))
+    kept = jnp.concatenate([split2(kept_e), split2(kept_h)], axis=0)
+    message = jnp.concatenate([dot(pack[...], kept)[:120], slot_stat[8:16]], axis=0)
+    hand_out[1] = message.T.reshape(n_dom, cap, RK)
+    handed_kept = exchange(hand_out.at[1], hand_in.at[1], hand_send.at[1], hand_recv.at[1])
+
     code_row = jnp.concatenate(codes, axis=1) >> 2
     fine_own[...] = one_hot(fine, code_row)
-    fine_halo[...] = one_hot(128, code_row - fine)
-    export_hot = one_hot(fine, export_row[...])
-    slot_hot = one_hot(slots, fine_slots[...])
-
-    finish(handed)
-    received = hand_in[...].reshape(slots, PK).T
-    received = dot(split2(received), slot_hot)
-    fine_stat = received[360:384] + received[PK + 360 : PK + 384]
-    state = dot(unpack[...], received.astype(bf16))
-    efield, hfield = state[:FR], state[FR : 2 * FR]
-    fine_held = (state[2 * FR : 2 * FR + TR], state[2 * FR + TR :])
+    fine_halo[...] = one_hot(2 * width, code_row - fine)
+    export_at = lax.broadcasted_iota(jnp.int32, (2 * width, fine), 1)
+    export_hot = jnp.where(export_at == export_rows[...], 1.0, 0.0).astype(bf16)
+    slot_hot = one_hot(slots, my_slots)
+    fine_out[...] = jnp.zeros(fine_out.shape, f32)
+
+    @pl.loop(0, count // CHUNK)
+    def _(i):
+        start = pl.multiple_of(i * CHUNK, CHUNK)
+        for f in range(4):
+            code = face_nbr[f : f + 1, pl.ds(start, CHUNK)]
+            coarse_hot[f, :, pl.ds(start, CHUNK)] = one_hot(full, code >> 2)
+
+    def take(message):
+        got = dot(split2(message.reshape(slots, RK).T), slot_hot)
+        state = dot(unpack[...], got.astype(bf16))
+        return state[:FR], state[FR:], got[120:RK] + got[RK + 120 :]
+
+    finish(handed_fields)
+    efield, hfield, stat_a = take(hand_in[0])
+    finish(extras)
+
+    def add_extra(d, value):
+        return value + dot(split2(extra_in[d]), slots_of(d, my_slots))
+
+    stat_c = lax.fori_loop(0, n_dom, add_extra, jnp.zeros((16, fine), f32))
+    stat_c = stat_c[:8] + stat_c[8:]
+    finish(handed_kept)
+    kept_e, kept_h, stat_b = take(hand_in[1])
+    fine_stat = jnp.concatenate([stat_a, stat_b, stat_c], axis=0)
     fine_geo, fine_ns = fine_stat[GEO : GEO + 9], fine_stat[NS : NS + 12]
-    lane = lax.broadcasted_iota(jnp.int32, (FR, 128), 1)
-    frozen_code = 4 * fine + 8 * width
-
-    def fine_rate(field, held, turn):
-        parts = split2(field)
-        export = dot(parts, export_hot)
-        fine_out[turn] = export[:FR] + export[FR:]
+
+    def fine_rate(field, kept, turn):
+        hi, lo = split(field)
+        parts = jnp.concatenate([hi, lo], axis=0).astype(bf16)
+        export = dot_t(export_hot, hi.astype(bf16)) + dot_t(export_hot, lo.astype(bf16))
+        fine_out[turn, 0, :, :FR] = export[:width]
+        fine_out[turn, 1, :, :FR] = export[width:]
         copies = to_neighbours(
-            fine_out.at[turn], fine_out.at[turn], fine_in.at[turn], fine_send.at[turn], fine_recv.at[turn]
+            fine_out.at[turn], fine_in.at[turn], fine_send.at[turn], fine_recv.at[turn]
         )
         near = dot(parts, fine_own[...])
         own = dot(sel[...], parts)
-        spin = curl(dot(dmat[...], split3(field)), fine_geo)
+        spin = curl(dot(dmat[...], split3(field)), fine_geo) + kept
         for copy in copies:
             copy.wait()
-        halo = jnp.where(lane < width, fine_in[turn, 0], fine_in[turn, 1])
+        halo = fine_in[turn].reshape(2 * width, 128).T[:FR]
         near = near + dot(split2(halo), fine_halo[...])
         traces = dot(sel[...], near.astype(bf16))
         fluxes = []
         for f in range(4):
             at = f * 3 * FN
             outside = pick_face(traces[:, f * fine : (f + 1) * fine], codes[f] & 3)
-            outside = jnp.where(codes[f] == frozen_code, held[at : at + 3 * FN], outside)
             fluxes += flux(outside - own[at : at + 3 * FN], fine_ns, f)
         return spin + dot(lmat[...], split3(jnp.concatenate(fluxes, axis=0)))
 
     fine_step = coarse_step / SUBSTEPS
     for substep in range(SUBSTEPS):
-        hfield = hfield - fine_step * fine_rate(efield, fine_held[0], 2 * substep)
-        efield = efield + fine_step * fine_rate(hfield, fine_held[1], 2 * substep + 1)
+        hfield = hfield - fine_step * fine_rate(efield, kept_e, 2 * substep)
+        efield = efield + fine_step * fine_rate(hfield, kept_h, 2 * substep + 1)
 
     result = jnp.concatenate([split2(efield), split2(hfield)], axis=0)
-    result = split2(dot(ret[...], result))
+    result = split2(dot(pack[...], result))
     result = dot_t(slot_hot, result)
     result = result[:, :RK] + result[:, RK:]
     back_out[...] = result.reshape(n_dom, cap, RK)
@@ -399,11 +442,12 @@
     finish(returned)
     came = back_in[...].reshape(slots, RK).T
     came = dot_t(split2(came), send_hot[...]).astype(bf16)
-    came = dot(back[...], came)
+    came = dot(unpack[...], came)
     merged_e = jnp.where(is_fine, came[:FR], own_e[...])
     merged_h = jnp.where(is_fine, came[FR:], own_h[...])
     own_e[...] = merged_e
     own_h[...] = merged_h
+    pool_e, pool_h = pool.at[: 2 * FR], pool.at[2 * FR : 4 * FR]
     pool_e[:, :count] = split2(merged_e)
 
     halo_lane = lax.broadcasted_iota(jnp.int32, (FR, 128), 1)
@@ -419,7 +463,7 @@
         fluxes = []
         for f in range(4):
             code = face_nbr[f : f + 1, window]
-            near = dot(pool[:, :reach], one_hot(reach, code >> 2)).astype(bf16)
+            near = dot(pool[:, :reach], coarse_hot[f, :reach, window]).astype(bf16)
             outside = pick_face(dot(sel[...], near), code & 3)
             mine = own[f * 3 * FN : (f + 1) * 3 * FN]
             wall = code == 4 * (start + place) + f
@@ -444,7 +488,6 @@
             pool_h[:, window] = split2(new)
 
     last = count - CHUNK
-    full = count + 128
     set_halo(pool_e, 0, halo_e)
 
     @pl.loop(0, 2)
@@ -453,9 +496,7 @@
 
     halo_out[1, 0] = own_h[:, count - 128 :]
     halo_out[1, 1] = own_h[:, :128]
-    halo_h = to_neighbours(
-        halo_out.at[1, 0], halo_out.at[1, 1], halo_in.at[1], halo_send.at[1], halo_recv.at[1]
-    )
+    halo_h = to_neighbours(halo_out.at[1], halo_in.at[1], halo_send.at[1], halo_recv.at[1])
 
     @pl.loop(1, count // CHUNK - 1)
     def _(i):
@@ -501,9 +542,7 @@
             constant_values=count,
         ).reshape(-1)
         fine_slots = fine_slots // group * cap + fine_slots % group
-    export_row = jnp.concatenate(
-        [export_rows[1], export_rows[0], jnp.full((128 - 2 * width,), -1, jnp.int32)]
-    )
+    export_rows = jnp.concatenate([export_rows[1], export_rows[0]])
     operands = [
         fields,
         geometry,
@@ -514,7 +553,7 @@
         face_nbr,
         send_rows[None],
         fine_slots[None],
-        export_row[None],
+        export_rows[:, None],
         fine_nbr,
         *[jnp.asarray(x) for x in tables()],
     ]
@@ -528,24 +567,33 @@
         scratch_shapes=[
             pltpu.VMEM((FR, count), f32),
             pltpu.VMEM((FR, count), f32),
-            pltpu.VMEM((2 * FR, count + 128), bf16),
-            pltpu.VMEM((2 * FR, count + 128), bf16),
+            pltpu.VMEM((4 * FR + 64, count + 128), bf16),
             pltpu.VMEM((32, count), f32),
+            pltpu.VMEM((16, fine), f32),
             pltpu.VMEM((count, slots), bf16),
+            pltpu.VMEM((4, count + 128, count), bf16),
             pltpu.VMEM((fine, 4 * fine), bf16),
-            pltpu.VMEM((128, 4 * fine), bf16),
+            pltpu.VMEM((2 * width, 4 * fine), bf16),
             pltpu.VMEM((224, 3 * FR), bf16),
             pltpu.VMEM((FR, 3 * TR), bf16),
-            pltpu.VMEM((n_dom, cap, PK), f32),
-            pltpu.VMEM((n_dom, cap, PK), f32),
+            pltpu.VMEM((n_dom, 8, 128), f32),
+            pltpu.VMEM((n_dom, 8, 128), f32),
+            pltpu.VMEM((n_dom, 8, 128), f32),
+            pltpu.VMEM((n_dom, 8, 128), f32),
+            pltpu.VMEM((2, n_dom, cap, RK), f32),
+            pltpu.VMEM((2, n_dom, cap, RK), f32),
             pltpu.VMEM((n_dom, cap, RK), f32),
             pltpu.VMEM((n_dom, cap, RK), f32),
-            pltpu.VMEM((turns, FR, 128), f32),
-            pltpu.VMEM((turns, 2, FR, 128), f32),
+            pltpu.VMEM((turns, 2, width, 128), f32),
+            pltpu.VMEM((turns, 2, width, 128), f32),
             pltpu.VMEM((2, 2, FR, 128), f32),
             pltpu.VMEM((2, 2, FR, 128), f32),
             dma((n_dom,)),
             dma((n_dom,)),
+            dma((n_dom,)),
+            dma((n_dom,)),
+            dma((2, n_dom)),
+            dma((2, n_dom)),
             dma((n_dom,)),
             dma((n_dom,)),
             dma((turns, 2)),

time: 92.9 us -> 84.9 us (0.914)
  Pallas kernels: 89.1 us -> 81.3 us
    pallas_call x1, Pallas kernels: 89.1 us -> 81.3 us  [per_device(): pl.pallas_call(functools.partial(kernel, n_dom, n_sub, width), out_shape=...]
where the time goes in v1:
time: 84.9 us; the launch traced here: 84.7 us
  Pallas kernels  81.3 us (96%)
  local copies, waits for them, and re-layouts  3.31 us (4%)
    pallas_call x1, Pallas kernels, per_device(): pl.pallas_call(functools.partial(kernel, n_dom, n_sub, width), out_shape=...  81.3 us
    unnamed x3, local copies, waits for them, and re-layouts  2.61 us

profile of v1, /device:TPU:0, one launch (start us, length us, event | category | flops | bytes accessed | tf_op | source)
XLA Modules:
  0.0 84.7 jit_solution(9279407548181544240)
XLA Ops:
  0.0 0.0 copy-start
  0.0 0.7 copy-done
  0.7 0.1 add_bitcast_fusion
  0.8 0.7 copy.23.export_rows
  1.5 81.3 %shard_map.208 = f32[6,20,1024]{2,1,0:T(8,128)} custom-call(f32[6,20,1024]{2,1,0:T(8,128)} %fields.1, f32[9,1024]{1,0:T(8,128)} %geometry.1, f32[3,4,1024]{2,1,0:T(4,128)} %normals.1, f32[4,1024]{1,0:T(4,128)} %face_scale.1, f32[3,20,20]{2,1,0:T(8,128)} %derivatives.1, f32[20,40]{1,0:T(8,128)} %lift_matrix.1, s32[4,1024]{1,0:T(4,128)} %face_nbr.1, ...), custom_call_target="tpu_custom_call" | custom-call | tf_op jit(solution)/shard_map/pallas_call | solution.py:562
  82.8 1.9 %copy.25 = f32[6,20,1024]{2,1,0:T(8,128)} copy(f32[6,20,1024]{2,1,0:T(8,128)} %shard_map.208) | data formatting | bytes 983040
  (1 shorter events, 0.0 us)
Async XLA Ops:
  0.0 0.7 copy-start

commit v2 on v1

--- a/solution.py
+++ b/solution.py
@@ -79,8 +79,8 @@
                 l_mask[c * PADC : c * PADC + 20, col : col + 10] = 0.5
                 for n in range(10):
                     (l_lo if s == 2 else l_hi)[f * 10 + n, col + n] = 1
-    out = [sel, pack, unpack, d_rows, d_hi, d_lo, l_rows, l_hi, l_lo]
-    return [x.astype(jnp.bfloat16) for x in out] + [d_mask, l_mask]
+    out = [unpack, d_rows, d_hi, d_lo, l_rows, l_hi, l_lo]
+    return [sel, pack] + [x.astype(jnp.bfloat16) for x in out] + [d_mask, l_mask]
 
 
 def split(x):
@@ -146,38 +146,44 @@
     ]
 
 
-def kernel(
-    n_dom,
-    n_sub,
-    width,
-    fields,
-    geometry,
-    normals,
-    face_scale,
-    derivatives,
-    lift_matrix,
-    face_nbr,
-    send_rows,
-    fine_slots,
-    export_rows,
-    fine_nbr,
-    sel,
-    pack,
-    unpack,
-    d_rows,
-    d_hi,
-    d_lo,
-    l_rows,
-    l_hi,
-    l_lo,
-    d_mask,
-    l_mask,
-    out,
+OPERANDS = 22
+
+
+def kernel(n_dom, n_sub, width, *refs):
+    given, out = refs[:OPERANDS], refs[OPERANDS]
+    local, load_sem = refs[OPERANDS + 1 : 2 * OPERANDS + 1], refs[2 * OPERANDS + 1]
+    (
+        fields,
+        geometry,
+        normals,
+        face_scale,
+        derivatives,
+        lift_matrix,
+        face_nbr,
+        send_rows,
+        fine_slots,
+        export_rows,
+        fine_nbr,
+        sel_full,
+        pack_full,
+        unpack,
+        d_rows,
+        d_hi,
+        d_lo,
+        l_rows,
+        l_hi,
+        l_lo,
+        d_mask,
+        l_mask,
+    ) = local
+    (
     own_e,
     own_h,
     pool,
     stat,
     frozen,
+    sel,
+    pack,
     send_hot,
     coarse_hot,
     fine_own,
@@ -208,7 +214,7 @@
     fine_recv,
     halo_send,
     halo_recv,
-):
+    ) = refs[2 * OPERANDS + 2 :]
     count = fields.shape[2]
     fine = fine_slots.shape[1]
     cap = hand_out.shape[2]
@@ -220,6 +226,15 @@
     after, before = lax.rem(me + 1, total), lax.rem(me + total - 1, total)
     after_id = (after // n_sub, lax.rem(after, n_sub))
     before_id = (before // n_sub, lax.rem(before, n_sub))
+
+    loads = [
+        pltpu.make_async_copy(src, dst, load_sem.at[i])
+        for i, (src, dst) in enumerate(zip(given, local))
+    ]
+    first_loads = [10, 8, 0]
+    later_loads = [i for i in range(OPERANDS) if i not in first_loads]
+    for i in first_loads + later_loads:
+        loads[i].start()
 
     barrier = pltpu.get_barrier_semaphore()
     for target in (after_id, before_id):
@@ -274,6 +289,9 @@
         at = lax.broadcasted_iota(jnp.int32, (128, row.shape[1]), 0)
         return jnp.where((row - d * cap == at) & (at < cap), 1.0, 0.0).astype(bf16)
 
+    for i in first_loads:
+        loads[i].wait()
+
     codes = [fine_nbr[f : f + 1, :] for f in range(4)]
     frozen_code = 4 * fine + 8 * width
     frozen[...] = jnp.zeros(frozen.shape, f32)
@@ -294,6 +312,12 @@
     pl.semaphore_wait(barrier, n_dom + 1)
     masks = exchange(mask_out, mask_in, mask_send, mask_recv)
     halo_e = to_neighbours(halo_out.at[0], halo_in.at[0], halo_send.at[0], halo_recv.at[0])
+
+    for i in later_loads:
+        loads[i].wait()
+
+    sel[...] = sel_full[...].astype(bf16)
+    pack[...] = pack_full[...].astype(bf16)
 
     stat[...] = jnp.zeros(stat.shape, f32)
     stat[GEO : GEO + 9, :] = geometry[...]
@@ -372,8 +396,10 @@
     code_row = jnp.concatenate(codes, axis=1) >> 2
     fine_own[...] = one_hot(fine, code_row)
     fine_halo[...] = one_hot(2 * width, code_row - fine)
-    export_at = lax.broadcasted_iota(jnp.int32, (2 * width, fine), 1)
-    export_hot = jnp.where(export_at == export_rows[...], 1.0, 0.0).astype(bf16)
+    eye = one_hot(width, lax.broadcasted_iota(jnp.int32, (1, width), 1))
+    export_hot = jnp.concatenate(
+        [dot_t(eye, one_hot(fine, export_rows[side : side + 1, :])) for side in (1, 0)], axis=0
+    ).astype(bf16)
     slot_hot = one_hot(slots, my_slots)
     fine_out[...] = jnp.zeros(fine_out.shape, f32)
 
@@ -542,7 +568,6 @@
             constant_values=count,
         ).reshape(-1)
         fine_slots = fine_slots // group * cap + fine_slots % group
-    export_rows = jnp.concatenate([export_rows[1], export_rows[0]])
     operands = [
         fields,
         geometry,
@@ -553,7 +578,7 @@
         face_nbr,
         send_rows[None],
         fine_slots[None],
-        export_rows[:, None],
+        export_rows,
         fine_nbr,
         *[jnp.asarray(x) for x in tables()],
     ]
@@ -562,14 +587,18 @@
     return pl.pallas_call(
         functools.partial(kernel, n_dom, n_sub, width),
         out_shape=jax.ShapeDtypeStruct(fields.shape, f32),
-        in_specs=[vmem] * len(operands),
+        in_specs=[pl.BlockSpec(memory_space=pl.ANY)] * len(operands),
         out_specs=vmem,
         scratch_shapes=[
+            *[pltpu.VMEM(x.shape, x.dtype) for x in operands],
+            dma((len(operands),)),
             pltpu.VMEM((FR, count), f32),
             pltpu.VMEM((FR, count), f32),
             pltpu.VMEM((4 * FR + 64, count + 128), bf16),
             pltpu.VMEM((32, count), f32),
             pltpu.VMEM((16, fine), f32),
+            pltpu.VMEM((TR, 2 * FR), bf16),
+            pltpu.VMEM((RK, 4 * FR), bf16),
             pltpu.VMEM((count, slots), bf16),
             pltpu.VMEM((4, count + 128, count), bf16),
             pltpu.VMEM((fine, 4 * fine), bf16),

time: 84.9 us -> 82.3 us (0.969)
  local copies, waits for them, and re-layouts: 3.31 us -> 1.93 us
  Pallas kernels: 81.3 us -> 80.1 us
    pallas_call x1, Pallas kernels: 81.3 us -> 80.1 us  [per_device(): pl.pallas_call(functools.partial(kernel, n_dom, n_sub, width), out_shape=...]
    unnamed x3 -> x1, local copies, waits for them, and re-layouts: 2.61 us -> 1.93 us
where the time goes in v2:
time: 82.3 us; the launch traced here: 82.1 us
  Pallas kernels  80.1 us (97%)
  local copies, waits for them, and re-layouts  1.93 us (2%)
    pallas_call x1, Pallas kernels, per_device(): pl.pallas_call(functools.partial(kernel, n_dom, n_sub, width), out_shape=...  80.1 us
    unnamed x1, local copies, waits for them, and re-layouts  1.93 us

profile of v2, /device:TPU:0, one launch (start us, length us, event | category | flops | bytes accessed | tf_op | source)
XLA Modules:
  0.0 82.1 jit_solution(14612059290228273222)
XLA Ops:
  0.0 80.1 %shard_map.208 = f32[6,20,1024]{2,1,0:T(8,128)} custom-call(f32[6,20,1024]{2,1,0:T(8,128)} %refs_0_.1, f32[9,1024]{1,0:T(8,128)} %refs_1_.1, f32[3,4,1024]{2,1,0:T(4,128)} %refs_2_.1, f32[4,1024]{1,0:T(4,128)} %refs_3_.1, f32[3,20,20]{2,1,0:T(8,128)} %refs_4_.1, f32[20,40]{1,0:T(8,128)} %refs_5_.1, s32[4,1024]{1,0:T(4,128)} %refs_6_.1, s32[1,512]{1,0:T(1,128)} %bitcast.2, ...), custom_call_target="tpu_custom_call" | custom-call | tf_op jit(solution)/shard_map/pallas_call | solution.py:587
  80.2 1.9 %copy.24 = f32[6,20,1024]{2,1,0:T(8,128)} copy(f32[6,20,1024]{2,1,0:T(8,128)} %shard_map.208) | data formatting | bytes 983040

commit v3 on v2

--- a/solution.py
+++ b/solution.py
@@ -188,6 +188,8 @@
     coarse_hot,
     fine_own,
     fine_halo,
+    tile_own,
+    tile_halo,
     dmat,
     lmat,
     mask_out,
@@ -198,6 +200,10 @@
     hand_in,
     back_out,
     back_in,
+    code_out,
+    code_in,
+    first_out,
+    first_in,
     fine_out,
     fine_in,
     halo_out,
@@ -210,6 +216,10 @@
     hand_recv,
     back_send,
     back_recv,
+    code_send,
+    code_recv,
+    first_send,
+    first_recv,
     fine_send,
     fine_recv,
     halo_send,
@@ -226,18 +236,21 @@
     after, before = lax.rem(me + 1, total), lax.rem(me + total - 1, total)
     after_id = (after // n_sub, lax.rem(after, n_sub))
     before_id = (before // n_sub, lax.rem(before, n_sub))
+    after2, before2 = lax.rem(me + 2, total), lax.rem(me + total - 2, total)
+    after2_id = (after2 // n_sub, lax.rem(after2, n_sub))
+    before2_id = (before2 // n_sub, lax.rem(before2, n_sub))
 
     loads = [
         pltpu.make_async_copy(src, dst, load_sem.at[i])
         for i, (src, dst) in enumerate(zip(given, local))
     ]
-    first_loads = [10, 8, 0]
+    first_loads = [10, 8, 9, 0]
     later_loads = [i for i in range(OPERANDS) if i not in first_loads]
     for i in first_loads + later_loads:
         loads[i].start()
 
     barrier = pltpu.get_barrier_semaphore()
-    for target in (after_id, before_id):
+    for target in (after_id, before_id, after2_id, before2_id):
         pl.semaphore_signal(barrier, inc=1, device_id=target, device_id_type=MESH)
 
     @pl.loop(1, n_dom)
@@ -296,7 +309,20 @@
     frozen_code = 4 * fine + 8 * width
     frozen[...] = jnp.zeros(frozen.shape, f32)
     frozen[0:4, :] = jnp.where(fine_nbr[...] == frozen_code, 1.0, 0.0)
+    frozen[4:8, :] = fine_nbr[...].astype(f32)
     my_slots = fine_slots[...]
+
+    eye = one_hot(width, lax.broadcasted_iota(jnp.int32, (1, width), 1))
+    export_up = dot_t(eye, one_hot(fine, export_rows[1:2, :])).astype(bf16)
+    export_down = dot_t(eye, one_hot(fine, export_rows[0:1, :])).astype(bf16)
+    export_hot = jnp.concatenate([export_up, export_down], axis=0)
+    code_row = jnp.concatenate(codes, axis=1) >> 2
+    fine_own[...] = one_hot(fine, code_row)
+    hi, lo = split(frozen[...])
+    exported = dot_t(export_hot, hi.astype(bf16)) + dot_t(export_hot, lo.astype(bf16))
+    code_out[...] = jnp.zeros(code_out.shape, f32)
+    code_out[0, :, :16] = exported[:width]
+    code_out[1, :, :16] = exported[width:]
 
     @pl.loop(0, n_dom)
     def _(d):
@@ -309,8 +335,9 @@
     halo_out[0, 0] = own_e[:, count - 128 :]
     halo_out[0, 1] = own_e[:, :128]
 
-    pl.semaphore_wait(barrier, n_dom + 1)
+    pl.semaphore_wait(barrier, n_dom + 3)
     masks = exchange(mask_out, mask_in, mask_send, mask_recv)
+    sent_codes = to_neighbours(code_out, code_in, code_send, code_recv)
     halo_e = to_neighbours(halo_out.at[0], halo_in.at[0], halo_send.at[0], halo_recv.at[0])
 
     for i in later_loads:
@@ -393,15 +420,53 @@
     hand_out[1] = message.T.reshape(n_dom, cap, RK)
     handed_kept = exchange(hand_out.at[1], hand_in.at[1], hand_send.at[1], hand_recv.at[1])
 
-    code_row = jnp.concatenate(codes, axis=1) >> 2
-    fine_own[...] = one_hot(fine, code_row)
-    fine_halo[...] = one_hot(2 * width, code_row - fine)
-    eye = one_hot(width, lax.broadcasted_iota(jnp.int32, (1, width), 1))
-    export_hot = jnp.concatenate(
-        [dot_t(eye, one_hot(fine, export_rows[side : side + 1, :])) for side in (1, 0)], axis=0
+    around_up = [dot_t(export_up, fine_own[:, f * fine : (f + 1) * fine]) for f in range(4)]
+    around_down = [dot_t(export_down, fine_own[:, f * fine : (f + 1) * fine]) for f in range(4)]
+    around = jnp.concatenate(
+        [*around_up, export_up.astype(f32), *around_down, export_down.astype(f32)], axis=0
     ).astype(bf16)
+    export_at = export_hot.astype(f32).T.astype(bf16)
+    pad_eye = one_hot(2 * width, lax.broadcasted_iota(jnp.int32, (1, fine), 1))
+    for copy in sent_codes:
+        copy.wait()
+    came_codes = dot(split2(code_in[...].reshape(2 * width, 128).T), pad_eye)
+    came_codes = (came_codes[:128] + came_codes[128:])[4:8].astype(jnp.int32)
+    ext = lax.broadcasted_iota(jnp.int32, (1, fine), 1)
+    below = ext < width
+    real = ext < 2 * width
+    low_end = 4 * fine + 4 * width
+    reach = 5 * width
+    codes_all = []
+    for f in range(4):
+        code = codes[f]
+        low, high = (code - 4 * fine) >> 2, (code - low_end) >> 2
+        at = jnp.where(code < low_end, 4 * width + low, reach + 4 * width + high)
+        at = jnp.where((code < 4 * fine) | (code >= frozen_code), -1, at)
+        code_x = came_codes[f : f + 1]
+        low, high = (code_x - 4 * fine) >> 2, (code_x - low_end) >> 2
+        is_near = code_x < 4 * fine
+        is_low = (code_x >= 4 * fine) & (code_x < low_end)
+        is_high = (code_x >= low_end) & (code_x < frozen_code)
+        at_x = jnp.where(below, f * width + ext, reach + f * width + ext - width)
+        at_x = jnp.where(is_near, at_x, -1)
+        at_x = jnp.where(is_low & below, 2 * reach + low, at_x)
+        at_x = jnp.where(is_high & (ext >= width), 2 * reach + width + high, at_x)
+        at_x = jnp.where(real, at_x, -1)
+        mine = jnp.where(is_low & (ext >= width), low, jnp.where(is_high & below, width + high, -1))
+        mine = jnp.where(real, mine, -1)
+        block = slice(2 * f * fine, (2 * f + 1) * fine)
+        block_x = slice((2 * f + 1) * fine, (2 * f + 2) * fine)
+        tile_own[:, block] = fine_own[:, f * fine : (f + 1) * fine]
+        tile_own[:, block_x] = dot(export_at, one_hot(2 * width, mine)).astype(bf16)
+        tile_halo[:, block] = one_hot(12 * width, at)
+        tile_halo[:, block_x] = one_hot(12 * width, at_x)
+        codes_all.append(jnp.concatenate([code, code_x], axis=1))
+    at = jnp.where(below, 4 * width + ext, reach + 4 * width + ext - width)
+    ext_hot = one_hot(12 * width, jnp.where(real, at, -1))
+    fine_halo[...] = one_hot(fine, code_row - fine)
+    fine_out[...] = jnp.zeros(fine_out.shape, f32)
+    first_out[...] = jnp.zeros(first_out.shape, f32)
     slot_hot = one_hot(slots, my_slots)
-    fine_out[...] = jnp.zeros(fine_out.shape, f32)
 
     @pl.loop(0, count // CHUNK)
     def _(i):
@@ -427,36 +492,83 @@
     finish(handed_kept)
     kept_e, kept_h, stat_b = take(hand_in[1])
     fine_stat = jnp.concatenate([stat_a, stat_b, stat_c], axis=0)
-    fine_geo, fine_ns = fine_stat[GEO : GEO + 9], fine_stat[NS : NS + 12]
-
-    def fine_rate(field, kept, turn):
-        hi, lo = split(field)
-        parts = jnp.concatenate([hi, lo], axis=0).astype(bf16)
-        export = dot_t(export_hot, hi.astype(bf16)) + dot_t(export_hot, lo.astype(bf16))
-        fine_out[turn, 0, :, :FR] = export[:width]
-        fine_out[turn, 1, :, :FR] = export[width:]
-        copies = to_neighbours(
-            fine_out.at[turn], fine_in.at[turn], fine_send.at[turn], fine_recv.at[turn]
+
+    def send_electric(parts, turn):
+        tile = dot_t(around, parts[:FR]) + dot_t(around, parts[FR:])
+        fine_out[turn, :, :FR] = tile
+        copies = []
+        plan = (
+            (after_id, 0, reach, 0),
+            (before_id, reach, reach, reach),
+            (after2_id, 4 * width, width, 2 * reach),
+            (before2_id, reach + 4 * width, width, 2 * reach + width),
         )
-        near = dot(parts, fine_own[...])
-        own = dot(sel[...], parts)
-        spin = curl(dot(dmat[...], split3(field)), fine_geo) + kept
-        for copy in copies:
-            copy.wait()
-        halo = fine_in[turn].reshape(2 * width, 128).T[:FR]
-        near = near + dot(split2(halo), fine_halo[...])
+        for side, (target, first, size, at) in enumerate(plan):
+            copy = pltpu.make_async_remote_copy(
+                src_ref=fine_out.at[turn, first : first + size],
+                dst_ref=fine_in.at[turn, at : at + size],
+                send_sem=fine_send.at[turn, side],
+                recv_sem=fine_recv.at[turn, side],
+                device_id=target,
+                device_id_type=MESH,
+            )
+            copy.start()
+            copies.append(copy)
+        return copies
+
+    def fluxes_of(near, own, face_codes, ns, size):
         traces = dot(sel[...], near.astype(bf16))
         fluxes = []
         for f in range(4):
             at = f * 3 * FN
-            outside = pick_face(traces[:, f * fine : (f + 1) * fine], codes[f] & 3)
-            fluxes += flux(outside - own[at : at + 3 * FN], fine_ns, f)
-        return spin + dot(lmat[...], split3(jnp.concatenate(fluxes, axis=0)))
+            outside = pick_face(traces[:, f * size : (f + 1) * size], face_codes[f] & 3)
+            fluxes += flux(outside - own[at : at + 3 * FN], ns, f)
+        return dot(lmat[...], split3(jnp.concatenate(fluxes, axis=0)))
 
     fine_step = coarse_step / SUBSTEPS
+    fine_geo, fine_ns = fine_stat[GEO : GEO + 9], fine_stat[NS : NS + 12]
     for substep in range(SUBSTEPS):
-        hfield = hfield - fine_step * fine_rate(efield, kept_e, 2 * substep)
-        efield = efield + fine_step * fine_rate(hfield, kept_h, 2 * substep + 1)
+        parts = split2(efield)
+        copies = send_electric(parts, substep)
+        if substep == 0:
+            start = jnp.concatenate([hfield, kept_e, fine_stat], axis=0)
+            hi, lo = split(start)
+            tile = dot_t(export_hot, hi.astype(bf16)) + dot_t(export_hot, lo.astype(bf16))
+            first_out[0, :, : tile.shape[1]] = tile[:width]
+            first_out[1, :, : tile.shape[1]] = tile[width:]
+            first_copies = to_neighbours(first_out, first_in, first_send, first_recv)
+        near = dot(parts, tile_own[...])
+        own = dot(sel[...], parts)
+        spin = curl(dot(dmat[...], split3(efield)), fine_geo)
+        if substep == 0:
+            for copy in first_copies:
+                copy.wait()
+            came = dot(split2(first_in[...].reshape(2 * width, 256).T), pad_eye)
+            came = came[:256] + came[256:]
+            hfield = jnp.concatenate([hfield, came[:FR]], axis=1)
+            kept_all = jnp.concatenate([kept_e, came[FR : 2 * FR]], axis=1)
+            stat_x = came[2 * FR : 2 * FR + 24]
+            geo_x = stat_x[GEO : GEO + 9]
+            ns_all = jnp.concatenate([fine_stat, stat_x], axis=1)[NS : NS + 12]
+        for copy in copies:
+            copy.wait()
+        halo = split2(fine_in[substep].T[:FR])
+        near = near + dot(halo, tile_halo[...])
+        parts_x = dot(halo, ext_hot)
+        field_x = parts_x[:FR] + parts_x[FR:]
+        own = jnp.concatenate([own, dot(sel[...], parts_x.astype(bf16))], axis=1)
+        spin_x = curl(dot(dmat[...], split3(field_x)), geo_x)
+        spin = jnp.concatenate([spin, spin_x], axis=1) + kept_all
+        rate = spin + fluxes_of(near, own, codes_all, ns_all, 2 * fine)
+        hfield = hfield - fine_step * rate
+
+        field = hfield[:, :fine]
+        parts = split2(field)
+        near = dot(parts, fine_own[...]) + dot(split2(hfield[:, fine:]), fine_halo[...])
+        own = dot(sel[...], parts)
+        spin = curl(dot(dmat[...], split3(field)), fine_geo) + kept_h
+        efield = efield + fine_step * (spin + fluxes_of(near, own, codes, fine_ns, fine))
+    hfield = hfield[:, :fine]
 
     result = jnp.concatenate([split2(efield), split2(hfield)], axis=0)
     result = split2(dot(pack[...], result))
@@ -560,7 +672,6 @@
     group = send_rows.shape[0] // n_dom
     cap = -(-group // 8) * 8
     slots = n_dom * cap
-    turns = 2 * SUBSTEPS
     if cap != group:
         send_rows = jnp.pad(
             send_rows.reshape(n_dom, group),
@@ -602,7 +713,9 @@
             pltpu.VMEM((count, slots), bf16),
             pltpu.VMEM((4, count + 128, count), bf16),
             pltpu.VMEM((fine, 4 * fine), bf16),
-            pltpu.VMEM((2 * width, 4 * fine), bf16),
+            pltpu.VMEM((fine, 4 * fine), bf16),
+            pltpu.VMEM((fine, 8 * fine), bf16),
+            pltpu.VMEM((12 * width, 8 * fine), bf16),
             pltpu.VMEM((224, 3 * FR), bf16),
             pltpu.VMEM((FR, 3 * TR), bf16),
             pltpu.VMEM((n_dom, 8, 128), f32),
@@ -613,8 +726,12 @@
             pltpu.VMEM((2, n_dom, cap, RK), f32),
             pltpu.VMEM((n_dom, cap, RK), f32),
             pltpu.VMEM((n_dom, cap, RK), f32),
-            pltpu.VMEM((turns, 2, width, 128), f32),
-            pltpu.VMEM((turns, 2, width, 128), f32),
+            pltpu.VMEM((2, width, 128), f32),
+            pltpu.VMEM((2, width, 128), f32),
+            pltpu.VMEM((2, width, 256), f32),
+            pltpu.VMEM((2, width, 256), f32),
+            pltpu.VMEM((SUBSTEPS, 10 * width, 128), f32),
+            pltpu.VMEM((SUBSTEPS, 12 * width, 128), f32),
             pltpu.VMEM((2, 2, FR, 128), f32),
             pltpu.VMEM((2, 2, FR, 128), f32),
             dma((n_dom,)),
@@ -625,8 +742,12 @@
             dma((2, n_dom)),
             dma((n_dom,)),
             dma((n_dom,)),
-            dma((turns, 2)),
-            dma((turns, 2)),
+            dma((2,)),
+            dma((2,)),
+            dma((2,)),
+            dma((2,)),
+            dma((SUBSTEPS, 4)),
+            dma((SUBSTEPS, 4)),
             dma((2, 2)),
             dma((2, 2)),
         ],

time: 82.3 us -> 71.1 us (0.86)
  Pallas kernels: 80.1 us -> 68.3 us
    pallas_call x1, Pallas kernels: 80.1 us -> 68.3 us  [per_device(): pl.pallas_call(functools.partial(kernel, n_dom, n_sub, width), out_shape=...]
where the time goes in v3:
time: 71.1 us; the launch traced here: 70.2 us
  Pallas kernels  68.3 us (96%)
  local copies, waits for them, and re-layouts  1.93 us (3%)
    pallas_call x1, Pallas kernels, per_device(): pl.pallas_call(functools.partial(kernel, n_dom, n_sub, width), out_shape=...  68.3 us
    unnamed x1, local copies, waits for them, and re-layouts  1.93 us

profile of v3, /device:TPU:0, one launch (start us, length us, event | category | flops | bytes accessed | tf_op | source)
XLA Modules:
  0.0 70.2 jit_solution(14813276897719143858)
XLA Ops:
  0.0 68.3 %shard_map.208 = f32[6,20,1024]{2,1,0:T(8,128)} custom-call(f32[6,20,1024]{2,1,0:T(8,128)} %refs_0_.1, f32[9,1024]{1,0:T(8,128)} %refs_1_.1, f32[3,4,1024]{2,1,0:T(4,128)} %refs_2_.1, f32[4,1024]{1,0:T(4,128)} %refs_3_.1, f32[3,20,20]{2,1,0:T(8,128)} %refs_4_.1, f32[20,40]{1,0:T(8,128)} %refs_5_.1, s32[4,1024]{1,0:T(4,128)} %refs_6_.1, s32[1,512]{1,0:T(1,128)} %bitcast.2, ...), custom_call_target="tpu_custom_call" | custom-call | tf_op jit(solution)/shard_map/pallas_call | solution.py:698
  68.3 1.9 %copy.24 = f32[6,20,1024]{2,1,0:T(8,128)} copy(f32[6,20,1024]{2,1,0:T(8,128)} %shard_map.208) | data formatting | bytes 983040

commit v4 on v3

--- a/solution.py
+++ b/solution.py
@@ -616,7 +616,6 @@
         pool[:, count:] = split2(pltpu.roll(tile, 64, 1))
 
     def update(start, source, pool, target, first, scale, reach, mirror):
-        start = pl.multiple_of(start, CHUNK)
         window = pl.ds(start, CHUNK)
         new = target[:, window] + scale * coarse_rate(start, source, pool, reach, mirror)
         target[:, window] = new
@@ -628,27 +627,22 @@
     last = count - CHUNK
     set_halo(pool_e, 0, halo_e)
 
-    @pl.loop(0, 2)
-    def _(i):
-        update(i * last, own_e, pool_e, own_h, 3, -coarse_step, full, -1.0)
+    for start in (0, last):
+        update(start, own_e, pool_e, own_h, 3, -coarse_step, full, -1.0)
 
     halo_out[1, 0] = own_h[:, count - 128 :]
     halo_out[1, 1] = own_h[:, :128]
     halo_h = to_neighbours(halo_out.at[1], halo_in.at[1], halo_send.at[1], halo_recv.at[1])
 
-    @pl.loop(1, count // CHUNK - 1)
-    def _(i):
-        update(i * CHUNK, own_e, pool_e, own_h, 3, -coarse_step, count, -1.0)
-
-    @pl.loop(1, count // CHUNK - 1)
-    def _(i):
-        update(i * CHUNK, own_h, pool_h, own_e, 0, coarse_step, count, 1.0)
+    for start in range(CHUNK, last, CHUNK):
+        update(start, own_e, pool_e, own_h, 3, -coarse_step, count, -1.0)
+    for start in range(CHUNK, last, CHUNK):
+        update(start, own_h, pool_h, own_e, 0, coarse_step, count, 1.0)
 
     set_halo(pool_h, 1, halo_h)
 
-    @pl.loop(0, 2)
-    def _(i):
-        update(i * last, own_h, pool_h, own_e, 0, coarse_step, full, 1.0)
+    for start in (0, last):
+        update(start, own_h, pool_h, own_e, 0, coarse_step, full, 1.0)
 
 
 def per_device(
@@ -697,7 +691,7 @@
     dma = pltpu.SemaphoreType.DMA
     return pl.pallas_call(
         functools.partial(kernel, n_dom, n_sub, width),
-        out_shape=jax.ShapeDtypeStruct(fields.shape, f32),
+        out_shape=pltpu.VMEM(fields.shape, f32),
         in_specs=[pl.BlockSpec(memory_space=pl.ANY)] * len(operands),
         out_specs=vmem,
         scratch_shapes=[

time: 71.1 us -> 67.3 us (0.947)
  Pallas kernels: 68.3 us -> 65.5 us
  local copies, waits for them, and re-layouts: 1.93 us -> 0.82 us
    pallas_call x1, Pallas kernels: 68.3 us -> 65.5 us  [per_device(): pl.pallas_call(functools.partial(kernel, n_dom, n_sub, width), out_shape=...]
    unnamed x1, local copies, waits for them, and re-layouts: 1.93 us -> 0.82 us
where the time goes in v4:
time: 67.3 us; the launch traced here: 66.3 us
  Pallas kernels  65.5 us (97%)
  local copies, waits for them, and re-layouts  0.82 us (1%)
    pallas_call x1, Pallas kernels, per_device(): pl.pallas_call(functools.partial(kernel, n_dom, n_sub, width), out_shape=...  65.5 us

profile of v4, /device:TPU:0, one launch (start us, length us, event | category | flops | bytes accessed | tf_op | source)
XLA Modules:
  0.0 66.3 jit_solution(12446673008977379062)
XLA Ops:
  0.0 65.5 %shard_map.208 = f32[6,20,1024]{2,1,0:T(8,128)S(1)} custom-call(f32[6,20,1024]{2,1,0:T(8,128)} %refs_0_.1, f32[9,1024]{1,0:T(8,128)} %refs_1_.1, f32[3,4,1024]{2,1,0:T(4,128)} %refs_2_.1, f32[4,1024]{1,0:T(4,128)} %refs_3_.1, f32[3,20,20]{2,1,0:T(8,128)} %refs_4_.1, f32[20,40]{1,0:T(8,128)} %refs_5_.1, s32[4,1024]{1,0:T(4,128)} %refs_6_.1, ...), custom_call_target="tpu_custom_call" | custom-call | tf_op jit(solution)/shard_map/pallas_call | solution.py:692
  65.5 0.8 %copy.24 = f32[6,20,1024]{2,1,0:T(8,128)} copy(f32[6,20,1024]{2,1,0:T(8,128)S(1)} %shard_map.208) | data formatting | bytes 983040

commit v5 on v4

--- a/solution.py
+++ b/solution.py
@@ -186,6 +186,9 @@
     pack,
     send_hot,
     coarse_hot,
+    still,
+    moved,
+    moved_hot,
     fine_own,
     fine_halo,
     tile_own,
@@ -204,6 +207,8 @@
     code_in,
     first_out,
     first_in,
+    kept_out,
+    kept_in,
     fine_out,
     fine_in,
     halo_out,
@@ -220,6 +225,8 @@
     code_recv,
     first_send,
     first_recv,
+    kept_send,
+    kept_recv,
     fine_send,
     fine_recv,
     halo_send,
@@ -364,12 +371,12 @@
     hand_out[0] = message.T.reshape(n_dom, cap, RK)
     handed_fields = exchange(hand_out.at[0], hand_in.at[0], hand_send.at[0], hand_recv.at[0])
     slot_row = lax.broadcasted_iota(jnp.int32, (1, slots), 1)
-    extra = split2(slot_stat[16:24])
+    extra = split2(slot_stat[8:24])
 
     @pl.loop(0, n_dom)
     def _(d):
         part = dot_t(extra, slots_of(d, slot_row))
-        extra_out[d] = part[:8] + part[8:]
+        extra_out[d] = part[:16] + part[16:]
 
     extras = exchange(extra_out, extra_in, extra_send, extra_recv)
 
@@ -416,8 +423,7 @@
     kept_e = dot(lmat[...], split3(jnp.concatenate(kept_e, axis=0)))
     kept_h = dot(lmat[...], split3(jnp.concatenate(kept_h, axis=0)))
     kept = jnp.concatenate([split2(kept_e), split2(kept_h)], axis=0)
-    message = jnp.concatenate([dot(pack[...], kept)[:120], slot_stat[8:16]], axis=0)
-    hand_out[1] = message.T.reshape(n_dom, cap, RK)
+    hand_out[1] = dot(pack[...], kept).T.reshape(n_dom, cap, RK)
     handed_kept = exchange(hand_out.at[1], hand_in.at[1], hand_send.at[1], hand_recv.at[1])
 
     around_up = [dot_t(export_up, fine_own[:, f * fine : (f + 1) * fine]) for f in range(4)]
@@ -425,6 +431,68 @@
     around = jnp.concatenate(
         [*around_up, export_up.astype(f32), *around_down, export_down.astype(f32)], axis=0
     ).astype(bf16)
+    slot_hot = one_hot(slots, my_slots)
+    reach = 5 * width
+    fine_out[...] = jnp.zeros(fine_out.shape, f32)
+    first_out[...] = jnp.zeros(first_out.shape, f32)
+    slot_hot = one_hot(slots, my_slots)
+    kept_out[...] = jnp.zeros(kept_out.shape, f32)
+
+    def take(message):
+        got = dot(split2(message.reshape(slots, RK).T), slot_hot)
+        state = dot(unpack[...], got.astype(bf16))
+        return state[:FR], state[FR:], got[120:RK] + got[RK + 120 :]
+
+    finish(handed_fields)
+    efield, hfield, stat_a = take(hand_in[0])
+    finish(extras)
+
+    def add_extra(d, value):
+        return value + dot(split2(extra_in[d]), slots_of(d, my_slots))
+
+    stat_c = lax.fori_loop(0, n_dom, add_extra, jnp.zeros((32, fine), f32))
+    stat_c = stat_c[:16] + stat_c[16:]
+    fine_stat = jnp.concatenate([stat_a, stat_c], axis=0)
+
+    def send_electric(parts, turn):
+        tile = dot_t(around, parts[:FR]) + dot_t(around, parts[FR:])
+        fine_out[turn, :, :FR] = tile
+        copies = []
+        plan = (
+            (after_id, 0, reach, 0),
+            (before_id, reach, reach, reach),
+            (after2_id, 4 * width, width, 2 * reach),
+            (before2_id, reach + 4 * width, width, 2 * reach + width),
+        )
+        for side, (target, first, size, at) in enumerate(plan):
+            copy = pltpu.make_async_remote_copy(
+                src_ref=fine_out.at[turn, first : first + size],
+                dst_ref=fine_in.at[turn, at : at + size],
+                send_sem=fine_send.at[turn, side],
+                recv_sem=fine_recv.at[turn, side],
+                device_id=target,
+                device_id_type=MESH,
+            )
+            copy.start()
+            copies.append(copy)
+        return copies
+
+    def fluxes_of(near, own, face_codes, ns, size):
+        traces = dot(sel[...], near.astype(bf16))
+        fluxes = []
+        for f in range(4):
+            at = f * 3 * FN
+            outside = pick_face(traces[:, f * size : (f + 1) * size], face_codes[f] & 3)
+            fluxes += flux(outside - own[at : at + 3 * FN], ns, f)
+        return dot(lmat[...], split3(jnp.concatenate(fluxes, axis=0)))
+
+    copies = send_electric(split2(efield), 0)
+    hi, lo = split(jnp.concatenate([hfield, fine_stat], axis=0))
+    tile = dot_t(export_hot, hi.astype(bf16)) + dot_t(export_hot, lo.astype(bf16))
+    first_out[0, :, : FR + 24] = tile[:width]
+    first_out[1, :, : FR + 24] = tile[width:]
+    first_copies = to_neighbours(first_out, first_in, first_send, first_recv)
+
     export_at = export_hot.astype(f32).T.astype(bf16)
     pad_eye = one_hot(2 * width, lax.broadcasted_iota(jnp.int32, (1, fine), 1))
     for copy in sent_codes:
@@ -464,9 +532,6 @@
     at = jnp.where(below, 4 * width + ext, reach + 4 * width + ext - width)
     ext_hot = one_hot(12 * width, jnp.where(real, at, -1))
     fine_halo[...] = one_hot(fine, code_row - fine)
-    fine_out[...] = jnp.zeros(fine_out.shape, f32)
-    first_out[...] = jnp.zeros(first_out.shape, f32)
-    slot_hot = one_hot(slots, my_slots)
 
     @pl.loop(0, count // CHUNK)
     def _(i):
@@ -475,79 +540,23 @@
             code = face_nbr[f : f + 1, pl.ds(start, CHUNK)]
             coarse_hot[f, :, pl.ds(start, CHUNK)] = one_hot(full, code >> 2)
 
-    def take(message):
-        got = dot(split2(message.reshape(slots, RK).T), slot_hot)
-        state = dot(unpack[...], got.astype(bf16))
-        return state[:FR], state[FR:], got[120:RK] + got[RK + 120 :]
-
-    finish(handed_fields)
-    efield, hfield, stat_a = take(hand_in[0])
-    finish(extras)
-
-    def add_extra(d, value):
-        return value + dot(split2(extra_in[d]), slots_of(d, my_slots))
-
-    stat_c = lax.fori_loop(0, n_dom, add_extra, jnp.zeros((16, fine), f32))
-    stat_c = stat_c[:8] + stat_c[8:]
-    finish(handed_kept)
-    kept_e, kept_h, stat_b = take(hand_in[1])
-    fine_stat = jnp.concatenate([stat_a, stat_b, stat_c], axis=0)
-
-    def send_electric(parts, turn):
-        tile = dot_t(around, parts[:FR]) + dot_t(around, parts[FR:])
-        fine_out[turn, :, :FR] = tile
-        copies = []
-        plan = (
-            (after_id, 0, reach, 0),
-            (before_id, reach, reach, reach),
-            (after2_id, 4 * width, width, 2 * reach),
-            (before2_id, reach + 4 * width, width, 2 * reach + width),
-        )
-        for side, (target, first, size, at) in enumerate(plan):
-            copy = pltpu.make_async_remote_copy(
-                src_ref=fine_out.at[turn, first : first + size],
-                dst_ref=fine_in.at[turn, at : at + size],
-                send_sem=fine_send.at[turn, side],
-                recv_sem=fine_recv.at[turn, side],
-                device_id=target,
-                device_id_type=MESH,
-            )
-            copy.start()
-            copies.append(copy)
-        return copies
-
-    def fluxes_of(near, own, face_codes, ns, size):
-        traces = dot(sel[...], near.astype(bf16))
-        fluxes = []
-        for f in range(4):
-            at = f * 3 * FN
-            outside = pick_face(traces[:, f * size : (f + 1) * size], face_codes[f] & 3)
-            fluxes += flux(outside - own[at : at + 3 * FN], ns, f)
-        return dot(lmat[...], split3(jnp.concatenate(fluxes, axis=0)))
 
     fine_step = coarse_step / SUBSTEPS
     fine_geo, fine_ns = fine_stat[GEO : GEO + 9], fine_stat[NS : NS + 12]
     for substep in range(SUBSTEPS):
         parts = split2(efield)
-        copies = send_electric(parts, substep)
-        if substep == 0:
-            start = jnp.concatenate([hfield, kept_e, fine_stat], axis=0)
-            hi, lo = split(start)
-            tile = dot_t(export_hot, hi.astype(bf16)) + dot_t(export_hot, lo.astype(bf16))
-            first_out[0, :, : tile.shape[1]] = tile[:width]
-            first_out[1, :, : tile.shape[1]] = tile[width:]
-            first_copies = to_neighbours(first_out, first_in, first_send, first_recv)
+        if substep > 0:
+            copies = send_electric(parts, substep)
         near = dot(parts, tile_own[...])
         own = dot(sel[...], parts)
         spin = curl(dot(dmat[...], split3(efield)), fine_geo)
         if substep == 0:
             for copy in first_copies:
                 copy.wait()
-            came = dot(split2(first_in[...].reshape(2 * width, 256).T), pad_eye)
-            came = came[:256] + came[256:]
+            came = dot(split2(first_in[...].reshape(2 * width, 128).T), pad_eye)
+            came = came[:128] + came[128:]
             hfield = jnp.concatenate([hfield, came[:FR]], axis=1)
-            kept_all = jnp.concatenate([kept_e, came[FR : 2 * FR]], axis=1)
-            stat_x = came[2 * FR : 2 * FR + 24]
+            stat_x = came[FR : FR + 24]
             geo_x = stat_x[GEO : GEO + 9]
             ns_all = jnp.concatenate([fine_stat, stat_x], axis=1)[NS : NS + 12]
         for copy in copies:
@@ -558,9 +567,20 @@
         field_x = parts_x[:FR] + parts_x[FR:]
         own = jnp.concatenate([own, dot(sel[...], parts_x.astype(bf16))], axis=1)
         spin_x = curl(dot(dmat[...], split3(field_x)), geo_x)
-        spin = jnp.concatenate([spin, spin_x], axis=1) + kept_all
-        rate = spin + fluxes_of(near, own, codes_all, ns_all, 2 * fine)
-        hfield = hfield - fine_step * rate
+        rate = jnp.concatenate([spin, spin_x], axis=1)
+        rate = rate + fluxes_of(near, own, codes_all, ns_all, 2 * fine)
+        if substep == 0:
+            finish(handed_kept)
+            kept_e, kept_h, _ = take(hand_in[1])
+            hi, lo = split(kept_e)
+            tile = dot_t(export_hot, hi.astype(bf16)) + dot_t(export_hot, lo.astype(bf16))
+            kept_out[0, :, :FR] = tile[:width]
+            kept_out[1, :, :FR] = tile[width:]
+            for copy in to_neighbours(kept_out, kept_in, kept_send, kept_recv):
+                copy.wait()
+            came = dot(split2(kept_in[...].reshape(2 * width, 128).T), pad_eye)
+            kept_all = jnp.concatenate([kept_e, came[:FR] + came[128 : 128 + FR]], axis=1)
+        hfield = hfield - fine_step * (rate + kept_all)
 
         field = hfield[:, :fine]
         parts = split2(field)
@@ -577,21 +597,43 @@
     back_out[...] = result.reshape(n_dom, cap, RK)
     returned = exchange(back_out, back_in, back_send, back_recv)
     is_fine = dot_t(jnp.ones((16, slots), bf16), send_hot[...])[:1] > 0.5
+    pool_e, pool_h = pool.at[: 2 * FR], pool.at[2 * FR : 4 * FR]
+    halo_lane = lax.broadcasted_iota(jnp.int32, (FR, 128), 1)
+
+    def set_halo(pool, turn, copies):
+        for copy in copies:
+            copy.wait()
+        tile = jnp.where(halo_lane < 64, halo_in[turn, 1], halo_in[turn, 0])
+        pool[:, count:] = split2(pltpu.roll(tile, 64, 1))
+
+    set_halo(pool_e, 0, halo_e)
+    pool_e[:, :count] = split2(jnp.where(is_fine, 0.0, own_e[...]))
+    slot_at = jnp.broadcast_to(rows.astype(f32), (8, slots)).T[:, :1].astype(jnp.int32)
+    slot_at = jnp.where(slot_at < count, slot_at, -1)
+
+    @pl.loop(0, count // CHUNK)
+    def _(i):
+        window = pl.ds(pl.multiple_of(i * CHUNK, CHUNK), CHUNK)
+        for f in range(4):
+            near = dot(pool_e[...], coarse_hot[f, :, window])
+            still[f, :, window] = near.astype(bf16)
+            code = face_nbr[f : f + 1, window] >> 2
+            moved_hot[f, :, window] = jnp.where(slot_at == code, 1.0, 0.0).astype(bf16)
+
     finish(returned)
     came = back_in[...].reshape(slots, RK).T
-    came = dot_t(split2(came), send_hot[...]).astype(bf16)
+    came = split2(came)
+    moved[...] = split2(dot(unpack[:FR], came))
+    came = dot_t(came, send_hot[...]).astype(bf16)
     came = dot(unpack[...], came)
     merged_e = jnp.where(is_fine, came[:FR], own_e[...])
     merged_h = jnp.where(is_fine, came[FR:], own_h[...])
     own_e[...] = merged_e
     own_h[...] = merged_h
-    pool_e, pool_h = pool.at[: 2 * FR], pool.at[2 * FR : 4 * FR]
-    pool_e[:, :count] = split2(merged_e)
-
-    halo_lane = lax.broadcasted_iota(jnp.int32, (FR, 128), 1)
+
     place = lax.broadcasted_iota(jnp.int32, (1, CHUNK), 1)
 
-    def coarse_rate(start, source, pool, reach, mirror):
+    def coarse_rate(start, source, gather, mirror):
         window = pl.ds(start, CHUNK)
         field = source[:, window]
         table = stat[:, window]
@@ -601,7 +643,7 @@
         fluxes = []
         for f in range(4):
             code = face_nbr[f : f + 1, window]
-            near = dot(pool[:, :reach], coarse_hot[f, :reach, window]).astype(bf16)
+            near = gather(f, window).astype(bf16)
             outside = pick_face(dot(sel[...], near), code & 3)
             mine = own[f * 3 * FN : (f + 1) * 3 * FN]
             wall = code == 4 * (start + place) + f
@@ -609,15 +651,15 @@
             fluxes += flux(outside - mine, ns, f)
         return spin + dot(lmat[...], split3(jnp.concatenate(fluxes, axis=0)))
 
-    def set_halo(pool, turn, copies):
-        for copy in copies:
-            copy.wait()
-        tile = jnp.where(halo_lane < 64, halo_in[turn, 1], halo_in[turn, 0])
-        pool[:, count:] = split2(pltpu.roll(tile, 64, 1))
-
-    def update(start, source, pool, target, first, scale, reach, mirror):
+    def electric_near(f, window):
+        return dot(moved[...], moved_hot[f, :, window]) + still[f, :, window].astype(f32)
+
+    def magnetic_near(reach):
+        return lambda f, window: dot(pool_h[:, :reach], coarse_hot[f, :reach, window])
+
+    def update(start, source, gather, target, first, scale, mirror):
         window = pl.ds(start, CHUNK)
-        new = target[:, window] + scale * coarse_rate(start, source, pool, reach, mirror)
+        new = target[:, window] + scale * coarse_rate(start, source, gather, mirror)
         target[:, window] = new
         for c in range(3):
             out[first + c, :, window] = new[c * PADC : c * PADC + 20]
@@ -625,24 +667,23 @@
             pool_h[:, window] = split2(new)
 
     last = count - CHUNK
-    set_halo(pool_e, 0, halo_e)
 
     for start in (0, last):
-        update(start, own_e, pool_e, own_h, 3, -coarse_step, full, -1.0)
+        update(start, own_e, electric_near, own_h, 3, -coarse_step, -1.0)
 
     halo_out[1, 0] = own_h[:, count - 128 :]
     halo_out[1, 1] = own_h[:, :128]
     halo_h = to_neighbours(halo_out.at[1], halo_in.at[1], halo_send.at[1], halo_recv.at[1])
 
     for start in range(CHUNK, last, CHUNK):
-        update(start, own_e, pool_e, own_h, 3, -coarse_step, count, -1.0)
+        update(start, own_e, electric_near, own_h, 3, -coarse_step, -1.0)
     for start in range(CHUNK, last, CHUNK):
-        update(start, own_h, pool_h, own_e, 0, coarse_step, count, 1.0)
+        update(start, own_h, magnetic_near(count), own_e, 0, coarse_step, 1.0)
 
     set_halo(pool_h, 1, halo_h)
 
     for start in (0, last):
-        update(start, own_h, pool_h, own_e, 0, coarse_step, full, 1.0)
+        update(start, own_h, magnetic_near(full), own_e, 0, coarse_step, 1.0)
 
 
 def per_device(
@@ -706,6 +747,9 @@
             pltpu.VMEM((RK, 4 * FR), bf16),
             pltpu.VMEM((count, slots), bf16),
             pltpu.VMEM((4, count + 128, count), bf16),
+            pltpu.VMEM((4, 2 * FR, count), bf16),
+            pltpu.VMEM((2 * FR, slots), bf16),
+            pltpu.VMEM((4, slots, count), bf16),
             pltpu.VMEM((fine, 4 * fine), bf16),
             pltpu.VMEM((fine, 4 * fine), bf16),
             pltpu.VMEM((fine, 8 * fine), bf16),
@@ -714,16 +758,18 @@
             pltpu.VMEM((FR, 3 * TR), bf16),
             pltpu.VMEM((n_dom, 8, 128), f32),
             pltpu.VMEM((n_dom, 8, 128), f32),
-            pltpu.VMEM((n_dom, 8, 128), f32),
-            pltpu.VMEM((n_dom, 8, 128), f32),
+            pltpu.VMEM((n_dom, 16, 128), f32),
+            pltpu.VMEM((n_dom, 16, 128), f32),
             pltpu.VMEM((2, n_dom, cap, RK), f32),
             pltpu.VMEM((2, n_dom, cap, RK), f32),
             pltpu.VMEM((n_dom, cap, RK), f32),
             pltpu.VMEM((n_dom, cap, RK), f32),
             pltpu.VMEM((2, width, 128), f32),
             pltpu.VMEM((2, width, 128), f32),
-            pltpu.VMEM((2, width, 256), f32),
-            pltpu.VMEM((2, width, 256), f32),
+            pltpu.VMEM((2, width, 128), f32),
+            pltpu.VMEM((2, width, 128), f32),
+            pltpu.VMEM((2, width, 128), f32),
+            pltpu.VMEM((2, width, 128), f32),
             pltpu.VMEM((SUBSTEPS, 10 * width, 128), f32),
             pltpu.VMEM((SUBSTEPS, 12 * width, 128), f32),
             pltpu.VMEM((2, 2, FR, 128), f32),
@@ -736,6 +782,8 @@
             dma((2, n_dom)),
             dma((n_dom,)),
             dma((n_dom,)),
+            dma((2,)),
+            dma((2,)),
             dma((2,)),
             dma((2,)),
             dma((2,)),

time: 67.3 us -> 70 us (1.040); the launches traced: 66.3 us -> 69.9 us
  Pallas kernels: 65.5 us -> 69 us
    pallas_call x1, Pallas kernels: 65.5 us -> 69 us  [per_device(): pl.pallas_call(functools.partial(kernel, n_dom, n_sub, width), out_shape=...]
where the time goes in v5:
time: 70 us; the launch traced here: 69.9 us
  Pallas kernels  69 us (99%)
  local copies, waits for them, and re-layouts  0.82 us (1%)
    pallas_call x1, Pallas kernels, per_device(): pl.pallas_call(functools.partial(kernel, n_dom, n_sub, width), out_shape=...  69 us

profile of v5, /device:TPU:0, one launch (start us, length us, event | category | flops | bytes accessed | tf_op | source)
XLA Modules:
  0.0 69.9 jit_solution(1506152365824894319)
XLA Ops:
  0.0 69.0 %shard_map.208 = f32[6,20,1024]{2,1,0:T(8,128)S(1)} custom-call(f32[6,20,1024]{2,1,0:T(8,128)} %refs_0_.1, f32[9,1024]{1,0:T(8,128)} %refs_1_.1, f32[3,4,1024]{2,1,0:T(4,128)} %refs_2_.1, f32[4,1024]{1,0:T(4,128)} %refs_3_.1, f32[3,20,20]{2,1,0:T(8,128)} %refs_4_.1, f32[20,40]{1,0:T(8,128)} %refs_5_.1, s32[4,1024]{1,0:T(4,128)} %refs_6_.1, ...), custom_call_target="tpu_custom_call" | custom-call | tf_op jit(solution)/shard_map/pallas_call | solution.py:733
  69.0 0.8 %copy.24 = f32[6,20,1024]{2,1,0:T(8,128)} copy(f32[6,20,1024]{2,1,0:T(8,128)S(1)} %shard_map.208) | data formatting | bytes 983040

commit v6 on v4

--- a/solution.py
+++ b/solution.py
@@ -41,6 +41,11 @@
 def tables():
     nodes = face_table()
     sel = np.zeros((TR, 2 * FR), np.float32)
+    narrow = np.zeros((128, 2 * FR), np.float32)
+    for s in range(2):
+        for c in range(3):
+            for p in range(20):
+                narrow[s * 64 + c * 20 + p, s * FR + c * PADC + p] = 1
     pack = np.zeros((RK, 4 * FR), np.float32)
     unpack = np.zeros((2 * FR, 2 * RK), np.float32)
     for c in range(3):
@@ -80,7 +85,7 @@
                 for n in range(10):
                     (l_lo if s == 2 else l_hi)[f * 10 + n, col + n] = 1
     out = [unpack, d_rows, d_hi, d_lo, l_rows, l_hi, l_lo]
-    return [sel, pack] + [x.astype(jnp.bfloat16) for x in out] + [d_mask, l_mask]
+    return [sel, pack, narrow] + [x.astype(jnp.bfloat16) for x in out] + [d_mask, l_mask]
 
 
 def split(x):
@@ -146,7 +151,7 @@
     ]
 
 
-OPERANDS = 22
+OPERANDS = 23
 
 
 def kernel(n_dom, n_sub, width, *refs):
@@ -166,6 +171,7 @@
         fine_nbr,
         sel_full,
         pack_full,
+        narrow_full,
         unpack,
         d_rows,
         d_hi,
@@ -184,6 +190,8 @@
     frozen,
     sel,
     pack,
+    narrow,
+    sel_narrow,
     send_hot,
     coarse_hot,
     fine_own,
@@ -345,6 +353,8 @@
 
     sel[...] = sel_full[...].astype(bf16)
     pack[...] = pack_full[...].astype(bf16)
+    narrow[...] = narrow_full[...].astype(bf16)
+    sel_narrow[...] = dot_t(sel[...], narrow[...]).astype(bf16)
 
     stat[...] = jnp.zeros(stat.shape, f32)
     stat[GEO : GEO + 9, :] = geometry[...]
@@ -585,8 +595,12 @@
     merged_h = jnp.where(is_fine, came[FR:], own_h[...])
     own_e[...] = merged_e
     own_h[...] = merged_h
-    pool_e, pool_h = pool.at[: 2 * FR], pool.at[2 * FR : 4 * FR]
-    pool_e[:, :count] = split2(merged_e)
+    pool_e, pool_h = pool.at[:128], pool.at[128:256]
+
+    def narrowed(x):
+        return dot(narrow[...], split2(x)).astype(bf16)
+
+    pool_e[:, :count] = narrowed(merged_e)
 
     halo_lane = lax.broadcasted_iota(jnp.int32, (FR, 128), 1)
     place = lax.broadcasted_iota(jnp.int32, (1, CHUNK), 1)
@@ -602,7 +616,7 @@
         for f in range(4):
             code = face_nbr[f : f + 1, window]
             near = dot(pool[:, :reach], coarse_hot[f, :reach, window]).astype(bf16)
-            outside = pick_face(dot(sel[...], near), code & 3)
+            outside = pick_face(dot(sel_narrow[...], near), code & 3)
             mine = own[f * 3 * FN : (f + 1) * 3 * FN]
             wall = code == 4 * (start + place) + f
             outside = jnp.where(wall, mirror * mine, outside)
@@ -613,7 +627,7 @@
         for copy in copies:
             copy.wait()
         tile = jnp.where(halo_lane < 64, halo_in[turn, 1], halo_in[turn, 0])
-        pool[:, count:] = split2(pltpu.roll(tile, 64, 1))
+        pool[:, count:] = narrowed(pltpu.roll(tile, 64, 1))
 
     def update(start, source, pool, target, first, scale, reach, mirror):
         window = pl.ds(start, CHUNK)
@@ -622,7 +636,7 @@
         for c in range(3):
             out[first + c, :, window] = new[c * PADC : c * PADC + 20]
         if first == 3:
-            pool_h[:, window] = split2(new)
+            pool_h[:, window] = narrowed(new)
 
     last = count - CHUNK
     set_halo(pool_e, 0, halo_e)
@@ -704,6 +718,8 @@
             pltpu.VMEM((16, fine), f32),
             pltpu.VMEM((TR, 2 * FR), bf16),
             pltpu.VMEM((RK, 4 * FR), bf16),
+            pltpu.VMEM((128, 2 * FR), bf16),
+            pltpu.VMEM((TR, 128), bf16),
             pltpu.VMEM((count, slots), bf16),
             pltpu.VMEM((4, count + 128, count), bf16),
             pltpu.VMEM((fine, 4 * fine), bf16),

time: 67.3 us -> 67.7 us (level)
  no operation moved by 1% of the time
where the time goes in v6:
time: 67.7 us; the launch traced here: 66.7 us
  Pallas kernels  65.9 us (97%)
  local copies, waits for them, and re-layouts  0.82 us (1%)
    pallas_call x1, Pallas kernels, per_device(): pl.pallas_call(functools.partial(kernel, n_dom, n_sub, width), out_shape=...  65.9 us

profile of v6, /device:TPU:0, one launch (start us, length us, event | category | flops | bytes accessed | tf_op | source)
XLA Modules:
  0.0 66.7 jit_solution(8035990745289498377)
XLA Ops:
  0.0 65.9 %shard_map.217 = f32[6,20,1024]{2,1,0:T(8,128)S(1)} custom-call(f32[6,20,1024]{2,1,0:T(8,128)} %refs_0_.1, f32[9,1024]{1,0:T(8,128)} %refs_1_.1, f32[3,4,1024]{2,1,0:T(4,128)} %refs_2_.1, f32[4,1024]{1,0:T(4,128)} %refs_3_.1, f32[3,20,20]{2,1,0:T(8,128)} %refs_4_.1, f32[20,40]{1,0:T(8,128)} %refs_5_.1, s32[4,1024]{1,0:T(4,128)} %refs_6_.1, ...), custom_call_target="tpu_custom_call" | custom-call | tf_op jit(solution)/shard_map/pallas_call | solution.py:706
  65.9 0.8 %copy.25 = f32[6,20,1024]{2,1,0:T(8,128)} copy(f32[6,20,1024]{2,1,0:T(8,128)S(1)} %shard_map.217) | data formatting | bytes 983040
